TPU v7x, 768 devices: a whole 4x8x12 slice. The times are simulated.
768 devices in a mesh: blk: 192 (over z, y_hi, x, core), group: 4 (over y_lo).
Axes of the slice: x: 4, y: 8 (y_hi: 2, y_lo: 4; y = y_hi * 4 + y_lo), z: 12, core: 2. Of those that a mesh axis runs over, the one named last changes fastest.
Arguments:
- images: bfloat16 [196608, 768], P('blk'), may hold values from -0.5 to 0.5
- captions: bfloat16 [196608, 768], P(('blk', 'group')), may hold values from -0.5 to 0.5
- pairing: int32 [192, 1024], P('blk', 'group'), may hold values from 0 to 1023, each once within a row
- logit_scale: float32 [1], replicated, may hold values from 5 to 15
- logit_bias: float32 [1], replicated, may hold values from -4 to -2
Outputs:
- image_grad: float32 [196608, 768], P(('blk', 'group'))
- caption_grad: float32 [196608, 768], P(('blk', 'group'))
- loss_rows: float32 [196608], P(('blk', 'group'))
Inputs may be any that keep to these rules, and one draw needn't show every extreme that they name: Each row of pairing is a permutation of 0 .. 1023.
All inputs are finite; a program needn't handle non-finite values.
Results may differ from a plain program's by a relative error of at most 0.0043.
Values may be sent and summed in bfloat16 or wider, within the bound.
No kernel may reach another device: no remote copies, remote signals or barrier semaphores. Data moves between devices by JAX's collectives and lax.ppermute only.
A program may use at most 32 MiB of HBM per device.

v0:
```python
import jax
import jax.numpy as jnp
from jax import lax
from jax.sharding import PartitionSpec as P

TOK_DEV = 256
STEPS = 4


def from_behind(block, axis, distance):
    devices = range(lax.axis_size(axis))
    route = [((i - distance) % len(devices), i) for i in devices]
    return lax.ppermute(block, axis, route)


def unit_rows(values):
    as_float = values.astype(jnp.float32)
    inverse = lax.rsqrt(jnp.sum(as_float * as_float, axis=-1, keepdims=True) + 1e-06)
    return (as_float * inverse, inverse)


def norm_back(unit, inverse, upstream):
    return inverse * (upstream - unit * jnp.sum(unit * upstream, axis=-1, keepdims=True))


def pair_terms(image_bf, visiting, scale_value, bias_value, label_signs):
    logits = (
        scale_value
        * lax.dot_general(
            image_bf, visiting, (((1,), (1,)), ((), ())), preferred_element_type=jnp.float32
        )
        + bias_value
    )
    loss_part = jnp.sum(jax.nn.softplus(-label_signs * logits), axis=1)
    pair_slope = (-label_signs * jax.nn.sigmoid(-label_signs * logits)).astype(jnp.bfloat16)
    image_term = scale_value * jnp.dot(pair_slope, visiting, preferred_element_type=jnp.float32)
    caption_term = scale_value * lax.dot_general(
        pair_slope, image_bf, (((0,), (0,)), ((), ())), preferred_element_type=jnp.float32
    )
    return (loss_part, image_term, caption_term)


def body(images, captions, pairing, logit_scale, logit_bias):
    image_unit, image_inv = unit_rows(images)
    caption_unit, caption_inv = unit_rows(captions)
    image_bf = image_unit.astype(jnp.bfloat16)
    caption_bf = caption_unit.astype(jnp.bfloat16)
    scale_value = logit_scale[0]
    bias_value = logit_bias[0]
    row_count = image_bf.shape[0]
    col_count = caption_bf.shape[0]
    positive = pairing[0][None, :] == lax.broadcasted_iota(jnp.int32, (row_count, col_count), 0)
    first_signs = jnp.where(positive, 1.0, -1.0).astype(jnp.float32)
    other_signs = -jnp.ones((row_count, col_count), jnp.float32)
    loss_sum, image_upstream, caption_upstream = pair_terms(
        image_bf, caption_bf, scale_value, bias_value, first_signs
    )
    visiting = caption_bf
    for offset in range(1, STEPS):
        visiting = from_behind(visiting, "blk", 1)
        loss_part, image_term, caption_term = pair_terms(
            image_bf, visiting, scale_value, bias_value, other_signs
        )
        loss_sum = loss_sum + loss_part
        image_upstream = image_upstream + image_term
        caption_upstream = from_behind(caption_upstream, "blk", 1) + caption_term
    caption_upstream = from_behind(caption_upstream, "blk", 1 - STEPS)
    image_share, loss_share = (
        lax.psum_scatter(image_upstream, "group", scatter_dimension=0, tiled=True),
        lax.psum_scatter(loss_sum, "group", scatter_dimension=0, tiled=True),
    )
    share_rows = image_share.shape[0]
    start = lax.axis_index("group") * share_rows
    own_unit = lax.dynamic_slice_in_dim(image_unit, start, share_rows, 0)
    own_inv = lax.dynamic_slice_in_dim(image_inv, start, share_rows, 0)
    image_grad = norm_back(own_unit, own_inv, image_share)
    caption_grad = norm_back(caption_unit, caption_inv, caption_upstream)
    loss_rows = loss_share / (STEPS * TOK_DEV)
    return (image_grad, caption_grad, loss_rows)


def solution(mesh):
    in_specs = (P("blk", None), P(("blk", "group"), None), P("blk", "group"), P(), P())
    out_specs = (P(("blk", "group"), None), P(("blk", "group"), None), P(("blk", "group")))
    return jax.shard_map(body, mesh=mesh, in_specs=in_specs, out_specs=out_specs, check_vma=False)
```

profile of v0, /device:TPU:397, one launch (start us, length us, event | category | flops | bytes accessed | tf_op | source)
XLA Modules:
  0.0 238.6 jit_solution(13120120139832393021)
XLA Ops:
  7.2 0.0 reduce-scatter.2.cloned.1.call-start
  7.2 1.2 fusion.17
  8.4 1.1 fusion.13
  9.5 3.4 %collective-permute-start = (bf16[256,768]{1,0:T(8,128)(2,1)S(1)}, bf16[256,768]{1,0:T(8,128)(2,1)S(1)}, u32[]{:S(2)}, u32[]{:S(2)}) collective-permute-start(bf16[256,768]{1,0:T(8,128)(2,1)S(1)} %fusion.13), channel_id=1, source_target_pairs={{764,0},{0,4},{4,8},{8,12},{12,16},{16,20},{20,24},{24,28},{28,32}... | collective-permute-start | bytes 1179656 | tf_op jit(solution)/shard_map/ppermute | solution.py:13
  14.2 1.8 fusion
  16.0 0.0 copy-start.2
  16.0 2.8 %fusion.7 = (f32[1024]{0:T(1024)S(1)}, f32[1024,256]{0,1:T(8,128)S(1)}) fusion(f32[]{:T(128)} %bitcast.21, bf16[256,768]{1,0:T(8,128)(2,1)S(1)} %fusion.13, f32[1024]{0:T(1024)S(1)} %add_rsqrt_fusion, bf16[1024,768]{1,0:T(8,128)(2,1)} %param.5, f32[]{:T(128)} %bitcast.13, s32[256]{0:T(256)} %bitcast.25), kind=kOutput, calls=%fused_computation.22 | convolution fusion | flops 408419328 | bytes 3023880 | tf_op jit(solution)/shard_map/dot_general | solution.py:29
  18.8 0.0 copy-start.7
  18.9 0.0 copy-start
  18.9 0.9 fusion.21
  19.8 0.0 copy-done.7
  19.8 0.0 collective-permute-done
  19.8 2.2 collective-permute-start.1
  22.0 1.9 fusion.8
  23.9 0.8 fusion.19
  24.7 2.0 collective-permute-done.1
  26.7 7.3 %collective-permute-start.2 = (bf16[256,768]{1,0:T(8,128)(2,1)S(1)}, bf16[256,768]{1,0:T(8,128)(2,1)S(1)}, u32[]{:S(2)}, u32[]{:S(2)}) collective-permute-start(bf16[256,768]{1,0:T(8,128)(2,1)S(1)} %collective-permute-done.1), channel_id=1, source_target_pairs={{764,0},{0,4},{4,8},{8,12},{12,16},{16,20},{20,24},{24,28},{28,32}... | collective-permute-start | bytes 1179656 | tf_op jit(solution)/shard_map/ppermute | solution.py:13
  34.0 1.9 fusion.9
  35.9 0.8 fusion.20
  36.7 2.0 collective-permute-done.2
  38.7 1.9 fusion.10
  40.6 2.5 %add_multiply_fusion = f32[1024,768]{1,0:T(8,128)} fusion(f32[1024,768]{1,0:T(8,128)S(1)} %fusion.20, f32[1024,768]{1,0:T(8,128)S(1)} %fusion.21, f32[1024,768]{1,0:T(8,128)S(1)} %fusion.19, bf16[256,768]{1,0:T(8,128)(2,1)S(1)} %collective-permute-done.2, f32[]{:T(128)} %bitcast.12, f32[1024,256]{0,1:T(8,128)S(1)} %get-tuple-element.4), kind=kOutput, calls=%fused_computation.3 | convolution fusion | flops 406847488 | bytes 14024708 | tf_op jit(solution)/shard_map/dot_general | solution.py:36
  43.1 0.0 reduce-scatter.2.cloned.1.call-update
  43.2 2.3 convolution_multiply_fusion.7
  45.4 15.6 %collective-permute-start.3 = (f32[256,768]{1,0:T(8,128)S(1)}, f32[256,768]{1,0:T(8,128)S(1)}, u32[]{:S(2)}, u32[]{:S(2)}) collective-permute-start(f32[256,768]{1,0:T(8,128)S(1)} %convolution_multiply_fusion.7), channel_id=1, source_target_pairs={{764,0},{0,4},{4,8},{8,12},{12,16},{16,20},{20,24},{24,28},{28,32}... | collective-permute-start | bytes 2359304 | tf_op jit(solution)/shard_map/ppermute | solution.py:13
  61.0 8.9 %collective-permute-done.3 = f32[256,768]{1,0:T(8,128)S(1)} collective-permute-done((f32[256,768]{1,0:T(8,128)S(1)}, f32[256,768]{1,0:T(8,128)S(1)}, u32[]{:S(2)}, u32[]{:S(2)}) %collective-permute-start.3) | collective-permute-done | bytes 786464 | tf_op jit(solution)/shard_map/ppermute | solution.py:13
  69.9 0.8 fusion.6
  70.8 9.6 %collective-permute-start.4 = (f32[256,768]{1,0:T(8,128)S(1)}, f32[256,768]{1,0:T(8,128)S(1)}, u32[]{:S(2)}, u32[]{:S(2)}) collective-permute-start(f32[256,768]{1,0:T(8,128)S(1)} %fusion.6), channel_id=1, source_target_pairs={{764,0},{0,4},{4,8},{8,12},{12,16},{16,20},{20,24},{24,28},{28,32}... | collective-permute-start | bytes 2359304 | tf_op jit(solution)/shard_map/ppermute | solution.py:13
  80.4 0.8 convolution_multiply_fusion.5
  81.2 8.1 %collective-permute-done.4 = f32[256,768]{1,0:T(8,128)S(1)} collective-permute-done((f32[256,768]{1,0:T(8,128)S(1)}, f32[256,768]{1,0:T(8,128)S(1)}, u32[]{:S(2)}, u32[]{:S(2)}) %collective-permute-start.4) | collective-permute-done | bytes 786464 | tf_op jit(solution)/shard_map/ppermute | solution.py:13
  89.3 0.1 add.123
  89.4 47.8 %collective-permute-start.5 = (f32[256,768]{1,0:T(8,128)S(1)}, f32[256,768]{1,0:T(8,128)S(1)}, u32[]{:S(2)}, u32[]{:S(2)}) collective-permute-start(f32[256,768]{1,0:T(8,128)S(1)} %add.123), channel_id=1, source_target_pairs={{764,0},{0,4},{4,8},{8,12},{12,16},{16,20},{20,24},{24,28},{28,32}... | collective-permute-start | bytes 2359304 | tf_op jit(solution)/shard_map/ppermute | solution.py:13
  137.2 0.8 convolution_multiply_fusion.4
  138.0 0.0 copy-start.1
  138.1 10.7 %collective-permute-done.5 = f32[256,768]{1,0:T(8,128)S(1)} collective-permute-done((f32[256,768]{1,0:T(8,128)S(1)}, f32[256,768]{1,0:T(8,128)S(1)}, u32[]{:S(2)}, u32[]{:S(2)}) %collective-permute-start.5) | collective-permute-done | bytes 786464 | tf_op jit(solution)/shard_map/ppermute | solution.py:13
  148.7 1.0 add.124
  149.7 1.9 collective-permute-start.6
  151.6 0.1 dynamic-slice.3
  151.7 1.3 dynamic-slice.4
  153.6 1.8 convert_multiply_fusion
  155.4 0.7 add_add_fusion
  156.1 4.8 %all-reduce = f32[1024]{0:T(1024)S(1)} all-reduce(f32[1024]{0:T(1024)S(1)} %add_add_fusion), channel_id=3, replica_groups=mesh['blk'=192,'group'=4] {'group'}, use_global_device_ids=true, to_apply=%region_9.10.clone | all-reduce | flops 1024 | bytes 8192
  160.9 0.6 dynamic-slice_multiply_fusion
  161.5 63.2 %collective-permute-done.6 = f32[256,768]{1,0:T(8,128)} collective-permute-done((f32[256,768]{1,0:T(8,128)}, f32[256,768]{1,0:T(8,128)}, u32[]{:S(2)}, u32[]{:S(2)}) %collective-permute-start.6) | collective-permute-done | bytes 786464 | tf_op jit(solution)/shard_map/ppermute | solution.py:13
  224.7 1.4 fusion.14
  226.1 2.2 fusion.16
  228.3 1.3 multiply_reduce_fusion
  229.6 2.2 subtract_multiply_fusion
  (14 shorter events, 0.0 us)
Async XLA Ops:
  7.2 221.2 %reduce-scatter.2.cloned.1.call-start = ((), (), s32[]{:S(2)}) async-start(), calls=%async_computation.1 | async-start | bytes 3932160 | tf_op jit(solution)/shard_map/reduce_scatter | solution.py:69
  9.5 10.3 %collective-permute-start = (bf16[256,768]{1,0:T(8,128)(2,1)S(1)}, bf16[256,768]{1,0:T(8,128)(2,1)S(1)}, u32[]{:S(2)}, u32[]{:S(2)}) collective-permute-start(bf16[256,768]{1,0:T(8,128)(2,1)S(1)} %fusion.13), channel_id=1, source_target_pairs={{764,0},{0,4},{4,8},{8,12},{12,16},{16,20},{20,24},{24,28},{28,32}... | collective-permute-start | bytes 1179656 | tf_op jit(solution)/shard_map/ppermute | solution.py:13
  16.0 2.8 %copy-start.2 = (s32[1,256]{1,0:T(1,128)S(1)}, s32[1,256]{1,0:T(1,128)}, u32[]{:S(2)}) copy-start(s32[1,256]{1,0:T(1,128)} %param.7) | copy-start | bytes 3076
  18.8 1.0 copy-start.7
  18.9 3.1 %copy-start = (bf16[1024,768]{1,0:T(8,128)(2,1)S(1)}, bf16[1024,768]{1,0:T(8,128)(2,1)}, u32[]{:S(2)}) copy-start(bf16[1024,768]{1,0:T(8,128)(2,1)} %param.5) | copy-start | bytes 4718596
  19.8 6.9 %collective-permute-start.1 = (bf16[256,768]{1,0:T(8,128)(2,1)S(1)}, bf16[256,768]{1,0:T(8,128)(2,1)S(1)}, u32[]{:S(2)}, u32[]{:S(2)}) collective-permute-start(bf16[256,768]{1,0:T(8,128)(2,1)S(1)} %collective-permute-done), channel_id=1, source_target_pairs={{764,0},{0,4},{4,8},{8,12},{12,16},{16,20},{20,24},{24,28},{28,32}... | collective-permute-start | bytes 1179656 | tf_op jit(solution)/shard_map/ppermute | solution.py:13
  23.9 12.0 %copy-start.3 = (f32[1024,256]{0,1:T(8,128)}, f32[1024,256]{0,1:T(8,128)S(1)}, u32[]{:S(2)}) copy-start(f32[1024,256]{0,1:T(8,128)S(1)} %get-tuple-element.10) | copy-start | bytes 3145732
  26.7 12.0 %collective-permute-start.2 = (bf16[256,768]{1,0:T(8,128)(2,1)S(1)}, bf16[256,768]{1,0:T(8,128)(2,1)S(1)}, u32[]{:S(2)}, u32[]{:S(2)}) collective-permute-start(bf16[256,768]{1,0:T(8,128)(2,1)S(1)} %collective-permute-done.1), channel_id=1, source_target_pairs={{764,0},{0,4},{4,8},{8,12},{12,16},{16,20},{20,24},{24,28},{28,32}... | collective-permute-start | bytes 1179656 | tf_op jit(solution)/shard_map/ppermute | solution.py:13
  35.9 4.7 %copy-start.5 = (f32[1024,256]{0,1:T(8,128)}, f32[1024,256]{0,1:T(8,128)S(1)}, u32[]{:S(2)}) copy-start(f32[1024,256]{0,1:T(8,128)S(1)} %get-tuple-element.6) | copy-start | bytes 3145732
  43.2 26.8 %copy-start.4 = (f32[1024,256]{0,1:T(8,128)S(1)}, f32[1024,256]{0,1:T(8,128)}, u32[]{:S(2)}) copy-start(f32[1024,256]{0,1:T(8,128)} %copy-done.3) | copy-start | bytes 3145732
  45.4 24.5 %collective-permute-start.3 = (f32[256,768]{1,0:T(8,128)S(1)}, f32[256,768]{1,0:T(8,128)S(1)}, u32[]{:S(2)}, u32[]{:S(2)}) collective-permute-start(f32[256,768]{1,0:T(8,128)S(1)} %convolution_multiply_fusion.7), channel_id=1, source_target_pairs={{764,0},{0,4},{4,8},{8,12},{12,16},{16,20},{20,24},{24,28},{28,32}... | collective-permute-start | bytes 2359304 | tf_op jit(solution)/shard_map/ppermute | solution.py:13
  69.9 10.4 %copy-start.6 = (f32[1024,256]{0,1:T(8,128)S(1)}, f32[1024,256]{0,1:T(8,128)}, u32[]{:S(2)}) copy-start(f32[1024,256]{0,1:T(8,128)} %copy-done.5) | copy-start | bytes 3145732
  70.8 18.5 %collective-permute-start.4 = (f32[256,768]{1,0:T(8,128)S(1)}, f32[256,768]{1,0:T(8,128)S(1)}, u32[]{:S(2)}, u32[]{:S(2)}) collective-permute-start(f32[256,768]{1,0:T(8,128)S(1)} %fusion.6), channel_id=1, source_target_pairs={{764,0},{0,4},{4,8},{8,12},{12,16},{16,20},{20,24},{24,28},{28,32}... | collective-permute-start | bytes 2359304 | tf_op jit(solution)/shard_map/ppermute | solution.py:13
  89.4 59.4 %collective-permute-start.5 = (f32[256,768]{1,0:T(8,128)S(1)}, f32[256,768]{1,0:T(8,128)S(1)}, u32[]{:S(2)}, u32[]{:S(2)}) collective-permute-start(f32[256,768]{1,0:T(8,128)S(1)} %add.123), channel_id=1, source_target_pairs={{764,0},{0,4},{4,8},{8,12},{12,16},{16,20},{20,24},{24,28},{28,32}... | collective-permute-start | bytes 2359304 | tf_op jit(solution)/shard_map/ppermute | solution.py:13
  138.0 86.7 %copy-start.1 = (bf16[256,768]{1,0:T(8,128)(2,1)S(1)}, bf16[256,768]{1,0:T(8,128)(2,1)}, u32[]{:S(2)}) copy-start(bf16[256,768]{1,0:T(8,128)(2,1)} %param.6) | copy-start | bytes 1179652
  149.7 75.0 %collective-permute-start.6 = (f32[256,768]{1,0:T(8,128)}, f32[256,768]{1,0:T(8,128)}, u32[]{:S(2)}, u32[]{:S(2)}) collective-permute-start(f32[256,768]{1,0:T(8,128)} %add.124), channel_id=1, source_target_pairs={{12,0},{16,4},{20,8},{24,12},{28,16},{32,20},{36,24},{40,28},{44,3... | collective-permute-start | bytes 2359304 | tf_op jit(solution)/shard_map/ppermute | solution.py:13
Sparse Core Ops, SparseCore 0:
  43.3 99.8 reduce-scatter.1
where the time goes:
time: 239 us
  waiting for transfers between devices  94.8 us (40%)
  starting transfers between devices  87.8 us (37%)
  matrix products  18.2 us (8%)
  between operations  16.2 us (7%)
  other arithmetic  15.3 us (6%)
  blocking collectives  4.78 us (2%)
    ppermute x7, waiting for transfers between devices, from_behind(): return lax.ppermute(block, axis, route)  94.8 us
    ppermute x7, starting transfers between devices, from_behind(): return lax.ppermute(block, axis, route)  87.8 us
    dot_general x4, matrix products, pair_terms(): lax.dot_general(image_bf, visiting, (((1,), (1,)), ((), ())), preferred_e...  8.49 us
    dot_general x4, matrix products, pair_terms(): jnp.dot(pair_slope, visiting, preferred_element_type=jnp.float32)  5.03 us
  transfers between devices with their start and end apart: 8, of which 6 were waited for; matrix products, arithmetic and copies ran while one was open for 10% of the time, Pallas kernels for 0%

commit v1 on v0

v1 whole, which is shorter than its diff:
```python
import jax
import jax.numpy as jnp
from jax import lax
from jax.sharding import PartitionSpec as P

TOK_DEV = 256
STEPS = 4
AXES = ("blk", "group")
ROW = 8
PAD = 16


def unit_rows(values):
    as_float = values.astype(jnp.float32)
    inverse = lax.rsqrt(jnp.sum(as_float * as_float, axis=-1, keepdims=True) + 1e-06)
    return (as_float * inverse, inverse)


def norm_back(unit, inverse, upstream):
    return inverse * (upstream - unit * jnp.sum(unit * upstream, axis=-1, keepdims=True))


def ring_routes(n_blk, n_group):
    forward = []
    for b in range(n_blk):
        for g in range(n_group):
            t = (b + 1) % n_blk
            lane = n_group - 1 - g if t // ROW != b // ROW else g
            forward.append((b * n_group + g, t * n_group + lane))
    return forward, [(t, s) for s, t in forward]


def group_routes(n_blk, n_group, pairs):
    return [(b * n_group + s, b * n_group + t) for b in range(n_blk) for s, t in pairs]


def pair_terms(image_bf, visiting, scale_value, bias_value, label_signs):
    logits = (
        scale_value
        * lax.dot_general(
            image_bf, visiting, (((1,), (1,)), ((), ())), preferred_element_type=jnp.float32
        )
        + bias_value
    )
    signed = -label_signs * logits
    loss_part = jnp.sum(jax.nn.softplus(signed), axis=1)
    pair_slope = (-label_signs * jax.nn.sigmoid(signed)).astype(jnp.bfloat16)
    caption_term = scale_value * lax.dot_general(
        pair_slope, image_bf, (((0,), (0,)), ((), ())), preferred_element_type=jnp.float32
    )
    return loss_part, pair_slope, caption_term


def body(images, captions, pairing, logit_scale, logit_bias):
    n_blk, n_group = lax.axis_size("blk"), lax.axis_size("group")
    forward, backward = ring_routes(n_blk, n_group)
    lane = lax.axis_index("group")

    def send(block, route):
        return lax.ppermute(block, AXES, route)

    caption_unit, caption_inv = unit_rows(captions)
    caption_bf = caption_unit.astype(jnp.bfloat16)
    visits = [caption_bf]
    for _ in range(1, STEPS):
        visits.append(send(visits[-1], forward))
    image_unit, image_inv = unit_rows(images)
    image_bf = image_unit.astype(jnp.bfloat16)
    scale_value = logit_scale[0]
    bias_value = logit_bias[0]
    row_count = image_bf.shape[0]
    col_count = caption_bf.shape[0]
    positive = pairing[0][None, :] == lax.broadcasted_iota(jnp.int32, (row_count, col_count), 0)
    signs = [jnp.where(positive, 1.0, -1.0).astype(jnp.float32)] + [jnp.float32(-1.0)] * 3
    losses, slopes, caption_terms = zip(
        *[pair_terms(image_bf, v, scale_value, bias_value, s) for v, s in zip(visits, signs)]
    )
    carried = caption_terms[3].astype(jnp.bfloat16)
    carried = send(carried, backward)
    carried = (carried.astype(jnp.float32) + caption_terms[2]).astype(jnp.bfloat16)
    carried = send(carried, backward)
    carried = (carried.astype(jnp.float32) + caption_terms[1]).astype(jnp.bfloat16)
    carried = send(carried, backward)
    caption_upstream = carried.astype(jnp.float32) + caption_terms[0]

    loss_sum = losses[0] + losses[1] + losses[2] + losses[3]
    image_term = scale_value * sum(
        jnp.dot(s, v, preferred_element_type=jnp.float32) for s, v in zip(slopes, visits)
    )
    share_rows = row_count // n_group
    loss_hi = loss_sum.astype(jnp.bfloat16)
    loss_lo = (loss_sum - loss_hi.astype(jnp.float32)).astype(jnp.bfloat16)
    tail = jnp.concatenate([loss_hi.reshape(n_group, 1, share_rows), loss_lo.reshape(n_group, 1, share_rows)], axis=1)
    tail = jnp.pad(tail, ((0, 0), (0, PAD - 2), (0, image_term.shape[1] - share_rows)))
    parts = jnp.concatenate(
        [image_term.astype(jnp.bfloat16).reshape(n_group, share_rows, -1), tail], axis=1
    )

    def part(table):
        at = jnp.asarray(table, jnp.int32)[lane]
        return lax.dynamic_index_in_dim(parts, at, 0, keepdims=False)

    def add(a, b):
        return (a.astype(jnp.float32) + b.astype(jnp.float32)).astype(jnp.bfloat16)

    carry = send(part([3, 0, 0, 0]), group_routes(n_blk, n_group, [(0, 1), (3, 2)]))
    near = send(part([1, 0, 3, 2]), group_routes(n_blk, n_group, [(0, 1), (1, 0), (2, 3), (3, 2)]))
    middle = send(part([0, 2, 1, 0]), group_routes(n_blk, n_group, [(1, 2), (2, 1)]))
    far = send(
        add(part([2, 3, 0, 1]), carry), group_routes(n_blk, n_group, [(0, 2), (1, 3), (2, 0), (3, 1)])
    )
    pieces = [part([0, 1, 2, 3]), near, middle, far]
    share = sum(p.astype(jnp.float32) for p in pieces)
    image_share = share[:share_rows]
    loss_share = share[share_rows, :share_rows] + share[share_rows + 1, :share_rows]
    start = lane * share_rows
    own_unit = lax.dynamic_slice_in_dim(image_unit, start, share_rows, 0)
    own_inv = lax.dynamic_slice_in_dim(image_inv, start, share_rows, 0)
    image_grad = norm_back(own_unit, own_inv, image_share)
    caption_grad = norm_back(caption_unit, caption_inv, caption_upstream)
    loss_rows = loss_share / (STEPS * TOK_DEV)
    return (image_grad, caption_grad, loss_rows)


def solution(mesh):
    in_specs = (P("blk", None), P(("blk", "group"), None), P("blk", "group"), P(), P())
    out_specs = (P(("blk", "group"), None), P(("blk", "group"), None), P(("blk", "group")))
    return jax.shard_map(body, mesh=mesh, in_specs=in_specs, out_specs=out_specs, check_vma=False)
```

time: 239 us -> 126 us (0.53)
  the two profiles are of different devices: /device:TPU:397 before, /device:TPU:1 now
where the time goes in v1:
time: 126 us; the launch traced here: 125 us
  starting transfers between devices  45.4 us (36%)
  waiting for transfers between devices  40.5 us (32%)
  matrix products  14.3 us (11%)
  other arithmetic  11.6 us (9%)
  between operations  9.85 us (8%)
  local copies, waits for them, and re-layouts  3.19 us (3%)
    ppermute x10, starting transfers between devices, send(): return lax.ppermute(block, AXES, route)  45.4 us
    ppermute x10, waiting for transfers between devices, send(): return lax.ppermute(block, AXES, route)  40.5 us
    dot_general x4, matrix products, pair_terms(): lax.dot_general(pair_slope, image_bf, (((0,), (0,)), ((), ())), preferred...  5.55 us
    dot_general x4, matrix products, pair_terms(): lax.dot_general(image_bf, visiting, (((1,), (1,)), ((), ())), preferred_e...  5.25 us
    dot_general x4, matrix products, body(): jnp.dot(s, v, preferred_element_type=jnp.float32)  3.5 us
    reduce_sum x2, other arithmetic, unit_rows(): jnp.sum(as_float * as_float, axis=-1, keepdims=True) + 1e-06  3.05 us
  transfers between devices with their start and end apart: 10, of which 4 were waited for; matrix products, arithmetic and copies ran while one was open for 17% of the time, Pallas kernels for 0%

profile of v1, /device:TPU:1, one launch (start us, length us, event | category | flops | bytes accessed | tf_op | source)
XLA Modules:
  0.0 124.9 jit_solution(355870166476916009)
XLA Ops:
  0.7 1.3 %fusion.20 = f32[256]{0:T(256)S(1)} fusion(bf16[256,768]{1,0:T(8,128)(2,1)} %param.11), kind=kLoop, calls=%fused_computation.55 | loop fusion | flops 589568 | bytes 394240 | tf_op jit(solution)/shard_map/reduce_sum | solution.py:15
  1.9 1.1 fusion.13
  3.1 4.5 %collective-permute-start = (bf16[256,768]{1,0:T(8,128)(2,1)S(1)}, bf16[256,768]{1,0:T(8,128)(2,1)S(1)}, u32[]{:S(2)}, u32[]{:S(2)}) collective-permute-start(bf16[256,768]{1,0:T(8,128)(2,1)S(1)} %fusion.13), channel_id=1, source_target_pairs={{0,4},{1,5},{2,6},{3,7},{4,8},{5,9},{6,10},{7,11},{8,12},{9,13},{1... | collective-permute-start | bytes 1179656 | tf_op jit(solution)/shard_map/ppermute | solution.py:60
  7.6 1.8 %fusion = f32[1024]{0:T(1024)S(1)} fusion(bf16[1024,768]{1,0:T(8,128)(2,1)} %param.10), kind=kLoop, calls=%fused_computation.7 | loop fusion | flops 2358272 | bytes 1576960 | tf_op jit(solution)/shard_map/reduce_sum | solution.py:15
  10.7 0.0 copy-start.6
  10.7 0.0 copy-start.5
  10.7 1.4 %fusion.7 = (f32[1024]{0:T(1024)S(1)}, f32[1024,256]{0,1:T(8,128)S(1)}) fusion(f32[]{:T(128)} %bitcast.43, bf16[256,768]{1,0:T(8,128)(2,1)S(1)} %fusion.13, f32[1024]{0:T(1024)S(1)} %add_rsqrt_fusion, bf16[1024,768]{1,0:T(8,128)(2,1)S(1)} %copy-done.1, f32[]{:T(128)} %bitcast.35, s32[256]{0:T(256)S(1)} %bitcast.53), kind=kOutput, calls=%fused_computation.32 | convolution fusion | flops 408419328 | bytes 3023880 | tf_op jit(solution)/shard_map/dot_general | solution.py:40
  12.2 0.7 dynamic_slice.39
  14.2 0.6 dynamic_slice.43
  15.9 0.6 dynamic_slice.37
  19.6 0.9 fusion.41
  20.6 1.9 %collective-permute-start.1 = (bf16[256,768]{1,0:T(8,128)(2,1)S(1)}, bf16[256,768]{1,0:T(8,128)(2,1)S(1)}, u32[]{:S(2)}, u32[]{:S(2)}) collective-permute-start(bf16[256,768]{1,0:T(8,128)(2,1)S(1)} %collective-permute-done), channel_id=1, source_target_pairs={{0,4},{1,5},{2,6},{3,7},{4,8},{5,9},{6,10},{7,11},{8,12},{9,13},{1... | collective-permute-start | bytes 1179656 | tf_op jit(solution)/shard_map/ppermute | solution.py:60
  22.5 1.3 %fusion.8 = (f32[1024]{0:T(1024)S(1)}, f32[1024,256]{0,1:T(8,128)S(1)}) fusion(f32[]{:T(128)} %bitcast.46, bf16[256,768]{1,0:T(8,128)(2,1)S(1)} %collective-permute-done, f32[1024]{0:T(1024)S(1)} %add_rsqrt_fusion, bf16[1024,768]{1,0:T(8,128)(2,1)S(1)} %copy-done.1, f32[]{:T(128)} %bitcast.39), kind=kOutput, calls=%fused_computation.33 | convolution fusion | flops 407370752 | bytes 3022856 | tf_op jit(solution)/shard_map/dot_general | solution.py:40
  23.8 0.8 fusion.39
  24.6 0.2 copy-done.8
  24.8 10.8 %collective-permute-done.1 = bf16[256,768]{1,0:T(8,128)(2,1)S(1)} collective-permute-done((bf16[256,768]{1,0:T(8,128)(2,1)S(1)}, bf16[256,768]{1,0:T(8,128)(2,1)S(1)}, u32[]{:S(2)}, u32[]{:S(2)}) %collective-permute-start.1) | collective-permute-done | bytes 393248 | tf_op jit(solution)/shard_map/ppermute | solution.py:60
  35.5 1.9 %collective-permute-start.2 = (bf16[256,768]{1,0:T(8,128)(2,1)S(1)}, bf16[256,768]{1,0:T(8,128)(2,1)S(1)}, u32[]{:S(2)}, u32[]{:S(2)}) collective-permute-start(bf16[256,768]{1,0:T(8,128)(2,1)S(1)} %collective-permute-done.1), channel_id=1, source_target_pairs={{0,4},{1,5},{2,6},{3,7},{4,8},{5,9},{6,10},{7,11},{8,12},{9,13},{1... | collective-permute-start | bytes 1179656 | tf_op jit(solution)/shard_map/ppermute | solution.py:60
  37.4 1.3 %fusion.9 = (f32[1024]{0:T(1024)S(1)}, f32[1024,256]{0,1:T(8,128)S(1)}) fusion(f32[]{:T(128)} %bitcast.45, bf16[256,768]{1,0:T(8,128)(2,1)S(1)} %collective-permute-done.1, f32[1024]{0:T(1024)S(1)} %add_rsqrt_fusion, bf16[1024,768]{1,0:T(8,128)(2,1)S(1)} %copy-done.1, f32[]{:T(128)} %bitcast.38), kind=kOutput, calls=%fused_computation.34 | convolution fusion | flops 407370752 | bytes 3022856 | tf_op jit(solution)/shard_map/dot_general | solution.py:40
  38.7 0.8 fusion.40
  39.5 0.2 copy-done.10
  39.7 11.6 %collective-permute-done.2 = bf16[256,768]{1,0:T(8,128)(2,1)S(1)} collective-permute-done((bf16[256,768]{1,0:T(8,128)(2,1)S(1)}, bf16[256,768]{1,0:T(8,128)(2,1)S(1)}, u32[]{:S(2)}, u32[]{:S(2)}) %collective-permute-start.2) | collective-permute-done | bytes 393248 | tf_op jit(solution)/shard_map/ppermute | solution.py:60
  51.3 1.3 %fusion.10 = (f32[1024]{0:T(1024)S(1)}, f32[1024,256]{0,1:T(8,128)S(1)}) fusion(f32[]{:T(128)} %bitcast.44, bf16[256,768]{1,0:T(8,128)(2,1)S(1)} %collective-permute-done.2, f32[1024]{0:T(1024)S(1)} %add_rsqrt_fusion, bf16[1024,768]{1,0:T(8,128)(2,1)S(1)} %copy-done.1, f32[]{:T(128)} %bitcast.37), kind=kOutput, calls=%fused_computation.35 | convolution fusion | flops 407370752 | bytes 3022856 | tf_op jit(solution)/shard_map/dot_general | solution.py:40
  52.7 1.6 %fusion.6 = bf16[256,768]{1,0:T(8,128)(2,1)} fusion(f32[]{:T(128)} %bitcast.36, f32[1024,256]{0,1:T(8,128)S(1)} %get-tuple-element.7, f32[1024]{0:T(1024)S(1)} %add_rsqrt_fusion, bf16[1024,768]{1,0:T(8,128)(2,1)S(1)} %copy-done.1), kind=kOutput, calls=%fused_computation.26 | convolution fusion | flops 406454272 | bytes 3018756 | tf_op jit(solution)/shard_map/dot_general | solution.py:48
  54.2 13.3 %collective-permute-start.7 = (bf16[256,768]{1,0:T(8,128)(2,1)}, bf16[256,768]{1,0:T(8,128)(2,1)}, u32[]{:S(2)}, u32[]{:S(2)}) collective-permute-start(bf16[256,768]{1,0:T(8,128)(2,1)} %fusion.6), channel_id=1, source_target_pairs={{4,0},{5,1},{6,2},{7,3},{8,4},{9,5},{10,6},{11,7},{12,8},{13,9},{1... | collective-permute-start | bytes 1179656 | tf_op jit(solution)/shard_map/ppermute | solution.py:60
  67.6 1.0 multiply_convert_fusion
  68.5 1.1 fusion.26
  69.6 8.9 %collective-permute-start.5 = (bf16[272,768]{1,0:T(8,128)(2,1)}, bf16[272,768]{1,0:T(8,128)(2,1)}, u32[]{:S(2)}, u32[]{:S(2)}) collective-permute-start(bf16[272,768]{1,0:T(8,128)(2,1)} %get-tuple-element.5), channel_id=1, source_target_pairs={{0,1},{3,2},{4,5},{7,6},{8,9},{11,10},{12,13},{15,14},{16,17},{19,... | collective-permute-start | bytes 1253384 | tf_op jit(solution)/shard_map/ppermute | solution.py:60
  78.5 2.0 %convert_multiply_fusion = f32[1024,768]{1,0:T(8,128)} fusion(bf16[1024,768]{1,0:T(8,128)(2,1)S(1)} %copy-done.1, f32[1024]{0:T(1024)S(1)} %add_rsqrt_fusion), kind=kLoop, calls=%fused_computation.5 | loop fusion | flops 1572864 | bytes 4722688 | tf_op jit(solution)/shard_map/mul | solution.py:16
  80.5 0.6 dynamic_slice.41
  82.4 0.1 dynamic-slice.3
  83.1 1.9 %collective-permute-start.3 = (bf16[272,768]{1,0:T(8,128)(2,1)}, bf16[272,768]{1,0:T(8,128)(2,1)S(1)}, u32[]{:S(2)}, u32[]{:S(2)}) collective-permute-start(bf16[272,768]{1,0:T(8,128)(2,1)} %get-tuple-element.3), channel_id=1, source_target_pairs={{0,1},{1,0},{2,3},{3,2},{4,5},{5,4},{6,7},{7,6},{8,9},{9,8},{10,11... | collective-permute-start | bytes 1253384 | tf_op jit(solution)/shard_map/ppermute | solution.py:60
  85.0 0.7 collective-permute-start.4
  85.7 2.1 %add_convert_fusion.1 = bf16[256,768]{1,0:T(8,128)(2,1)S(1)} fusion(bf16[256,768]{1,0:T(8,128)(2,1)} %collective-permute-done.7, f32[]{:T(128)} %bitcast.42, f32[1024,256]{0,1:T(8,128)} %copy-done.10, f32[1024]{0:T(1024)S(1)} %add_rsqrt_fusion, bf16[1024,768]{1,0:T(8,128)(2,1)S(1)} %copy-done.1), kind=kOutput, calls=%fused_computation.58 | convolution fusion | flops 406847488 | bytes 3411972 | tf_op jit(solution)/shard_map/dot_general | solution.py:48
  87.9 2.3 %collective-permute-start.8 = (bf16[256,768]{1,0:T(8,128)(2,1)S(1)}, bf16[256,768]{1,0:T(8,128)(2,1)S(1)}, u32[]{:S(2)}, u32[]{:S(2)}) collective-permute-start(bf16[256,768]{1,0:T(8,128)(2,1)S(1)} %add_convert_fusion.1), channel_id=1, source_target_pairs={{4,0},{5,1},{6,2},{7,3},{8,4},{9,5},{10,6},{11,7},{12,8},{13,9},{1... | collective-permute-start | bytes 1179656 | tf_op jit(solution)/shard_map/ppermute | solution.py:60
  90.2 1.0 collective-permute-done.5
  91.3 1.1 fusion.14
  92.4 6.3 %collective-permute-start.6 = (bf16[272,768]{1,0:T(8,128)(2,1)S(1)}, bf16[272,768]{1,0:T(8,128)(2,1)S(1)}, u32[]{:S(2)}, u32[]{:S(2)}) collective-permute-start(bf16[272,768]{1,0:T(8,128)(2,1)S(1)} %fusion.14), channel_id=1, source_target_pairs={{0,2},{1,3},{2,0},{3,1},{4,6},{5,7},{6,4},{7,5},{8,10},{9,11},{10,... | collective-permute-start | bytes 1253384 | tf_op jit(solution)/shard_map/ppermute | solution.py:60
  98.7 0.8 convolution_multiply_fusion.5
  99.6 0.1 add_convert_fusion
  99.7 3.6 %collective-permute-start.9 = (bf16[256,768]{1,0:T(8,128)(2,1)S(1)}, bf16[256,768]{1,0:T(8,128)(2,1)S(1)}, u32[]{:S(2)}, u32[]{:S(2)}) collective-permute-start(bf16[256,768]{1,0:T(8,128)(2,1)S(1)} %add_convert_fusion), channel_id=1, source_target_pairs={{4,0},{5,1},{6,2},{7,3},{8,4},{9,5},{10,6},{11,7},{12,8},{13,9},{1... | collective-permute-start | bytes 1179656 | tf_op jit(solution)/shard_map/ppermute | solution.py:60
  103.3 17.1 %collective-permute-done.6 = bf16[272,768]{1,0:T(8,128)(2,1)S(1)} collective-permute-done((bf16[272,768]{1,0:T(8,128)(2,1)S(1)}, bf16[272,768]{1,0:T(8,128)(2,1)S(1)}, u32[]{:S(2)}, u32[]{:S(2)}) %collective-permute-start.6) | collective-permute-done | bytes 417824 | tf_op jit(solution)/shard_map/ppermute | solution.py:60
  120.4 0.2 fusion.16
  120.6 0.6 fusion.37
  121.2 0.2 multiply_reduce_fusion
  121.4 1.1 subtract_multiply_fusion
  122.4 0.3 copy-done.12
  122.7 1.0 fusion.17
  123.8 1.1 fusion.19
  (33 shorter events, 0.1 us)
Async XLA Ops:
  0.6 10.1 %copy-start.1 = (bf16[1024,768]{1,0:T(8,128)(2,1)S(1)}, bf16[1024,768]{1,0:T(8,128)(2,1)}, u32[]{:S(2)}) copy-start(bf16[1024,768]{1,0:T(8,128)(2,1)} %param.10) | copy-start | bytes 4718596
  0.6 10.1 %copy-start.3 = (s32[1,256]{1,0:T(1,128)S(1)}, s32[1,256]{1,0:T(1,128)}, u32[]{:S(2)}) copy-start(s32[1,256]{1,0:T(1,128)} %param.12) | copy-start | bytes 3076
  3.1 17.5 %collective-permute-start = (bf16[256,768]{1,0:T(8,128)(2,1)S(1)}, bf16[256,768]{1,0:T(8,128)(2,1)S(1)}, u32[]{:S(2)}, u32[]{:S(2)}) collective-permute-start(bf16[256,768]{1,0:T(8,128)(2,1)S(1)} %fusion.13), channel_id=1, source_target_pairs={{0,4},{1,5},{2,6},{3,7},{4,8},{5,9},{6,10},{7,11},{8,12},{9,13},{1... | collective-permute-start | bytes 1179656 | tf_op jit(solution)/shard_map/ppermute | solution.py:60
  10.7 1.5 %copy-start.7 = (s32[4]{0:T(128)S(1)}, s32[4]{0:T(128)}, u32[]{:S(2)}) copy-start(s32[4]{0:T(128)} %constant.56.clone) | copy-start | bytes 52
  10.7 3.5 %copy-start.6 = (s32[4]{0:T(128)S(1)}, s32[4]{0:T(128)}, u32[]{:S(2)}) copy-start(s32[4]{0:T(128)} %constant.54.clone) | copy-start | bytes 52
  10.7 5.2 %copy-start.5 = (s32[4]{0:T(128)S(1)}, s32[4]{0:T(128)}, u32[]{:S(2)}) copy-start(s32[4]{0:T(128)} %constant.55.clone) | copy-start | bytes 52
  12.2 8.4 %copy-start.11 = (f32[1024,256]{0,1:T(8,128)}, f32[1024,256]{0,1:T(8,128)S(1)}, u32[]{:S(2)}) copy-start(f32[1024,256]{0,1:T(8,128)S(1)} %get-tuple-element.11) | copy-start | bytes 3145732
  20.6 14.9 %collective-permute-start.1 = (bf16[256,768]{1,0:T(8,128)(2,1)S(1)}, bf16[256,768]{1,0:T(8,128)(2,1)S(1)}, u32[]{:S(2)}, u32[]{:S(2)}) collective-permute-start(bf16[256,768]{1,0:T(8,128)(2,1)S(1)} %collective-permute-done), channel_id=1, source_target_pairs={{0,4},{1,5},{2,6},{3,7},{4,8},{5,9},{6,10},{7,11},{8,12},{9,13},{1... | collective-permute-start | bytes 1179656 | tf_op jit(solution)/shard_map/ppermute | solution.py:60
  23.8 1.0 copy-start.8
  35.5 15.8 %collective-permute-start.2 = (bf16[256,768]{1,0:T(8,128)(2,1)S(1)}, bf16[256,768]{1,0:T(8,128)(2,1)S(1)}, u32[]{:S(2)}, u32[]{:S(2)}) collective-permute-start(bf16[256,768]{1,0:T(8,128)(2,1)S(1)} %collective-permute-done.1), channel_id=1, source_target_pairs={{0,4},{1,5},{2,6},{3,7},{4,8},{5,9},{6,10},{7,11},{8,12},{9,13},{1... | collective-permute-start | bytes 1179656 | tf_op jit(solution)/shard_map/ppermute | solution.py:60
  38.7 1.0 copy-start.10
  54.2 31.5 %collective-permute-start.7 = (bf16[256,768]{1,0:T(8,128)(2,1)}, bf16[256,768]{1,0:T(8,128)(2,1)}, u32[]{:S(2)}, u32[]{:S(2)}) collective-permute-start(bf16[256,768]{1,0:T(8,128)(2,1)} %fusion.6), channel_id=1, source_target_pairs={{4,0},{5,1},{6,2},{7,3},{8,4},{9,5},{10,6},{11,7},{12,8},{13,9},{1... | collective-permute-start | bytes 1179656 | tf_op jit(solution)/shard_map/ppermute | solution.py:60
  69.6 10.9 %copy-start.4 = (s32[4]{0:T(128)S(1)}, s32[4]{0:T(128)}, u32[]{:S(2)}) copy-start(s32[4]{0:T(128)} %constant.57.clone) | copy-start | bytes 52
  69.6 21.7 %collective-permute-start.5 = (bf16[272,768]{1,0:T(8,128)(2,1)}, bf16[272,768]{1,0:T(8,128)(2,1)}, u32[]{:S(2)}, u32[]{:S(2)}) collective-permute-start(bf16[272,768]{1,0:T(8,128)(2,1)} %get-tuple-element.5), channel_id=1, source_target_pairs={{0,1},{3,2},{4,5},{7,6},{8,9},{11,10},{12,13},{15,14},{16,17},{19,... | collective-permute-start | bytes 1253384 | tf_op jit(solution)/shard_map/ppermute | solution.py:60
  83.1 20.2 %collective-permute-start.3 = (bf16[272,768]{1,0:T(8,128)(2,1)}, bf16[272,768]{1,0:T(8,128)(2,1)S(1)}, u32[]{:S(2)}, u32[]{:S(2)}) collective-permute-start(bf16[272,768]{1,0:T(8,128)(2,1)} %get-tuple-element.3), channel_id=1, source_target_pairs={{0,1},{1,0},{2,3},{3,2},{4,5},{5,4},{6,7},{7,6},{8,9},{9,8},{10,11... | collective-permute-start | bytes 1253384 | tf_op jit(solution)/shard_map/ppermute | solution.py:60
  85.0 18.3 %collective-permute-start.4 = (bf16[272,768]{1,0:T(8,128)(2,1)}, bf16[272,768]{1,0:T(8,128)(2,1)S(1)}, u32[]{:S(2)}, u32[]{:S(2)}) collective-permute-start(bf16[272,768]{1,0:T(8,128)(2,1)} %get-tuple-element.4), channel_id=1, source_target_pairs={{1,2},{2,1},{5,6},{6,5},{9,10},{10,9},{13,14},{14,13},{17,18},{18,... | collective-permute-start | bytes 1253384 | tf_op jit(solution)/shard_map/ppermute | solution.py:60
  87.9 10.9 %copy-start.9 = (f32[1024,256]{0,1:T(8,128)S(1)}, f32[1024,256]{0,1:T(8,128)}, u32[]{:S(2)}) copy-start(f32[1024,256]{0,1:T(8,128)} %copy-done.8) | copy-start | bytes 3145732
  87.9 11.7 %collective-permute-start.8 = (bf16[256,768]{1,0:T(8,128)(2,1)S(1)}, bf16[256,768]{1,0:T(8,128)(2,1)S(1)}, u32[]{:S(2)}, u32[]{:S(2)}) collective-permute-start(bf16[256,768]{1,0:T(8,128)(2,1)S(1)} %add_convert_fusion.1), channel_id=1, source_target_pairs={{4,0},{5,1},{6,2},{7,3},{8,4},{9,5},{10,6},{11,7},{12,8},{13,9},{1... | collective-permute-start | bytes 1179656 | tf_op jit(solution)/shard_map/ppermute | solution.py:60
  92.4 28.0 %collective-permute-start.6 = (bf16[272,768]{1,0:T(8,128)(2,1)S(1)}, bf16[272,768]{1,0:T(8,128)(2,1)S(1)}, u32[]{:S(2)}, u32[]{:S(2)}) collective-permute-start(bf16[272,768]{1,0:T(8,128)(2,1)S(1)} %fusion.14), channel_id=1, source_target_pairs={{0,2},{1,3},{2,0},{3,1},{4,6},{5,7},{6,4},{7,5},{8,10},{9,11},{10,... | collective-permute-start | bytes 1253384 | tf_op jit(solution)/shard_map/ppermute | solution.py:60
  99.6 21.5 %copy-start = (f32[1024,768]{1,0:T(8,128)S(1)}, f32[1024,768]{1,0:T(8,128)}, u32[]{:S(2)}) copy-start(f32[1024,768]{1,0:T(8,128)} %convert_multiply_fusion) | copy-start | bytes 9437188
  99.7 22.8 %collective-permute-start.9 = (bf16[256,768]{1,0:T(8,128)(2,1)S(1)}, bf16[256,768]{1,0:T(8,128)(2,1)S(1)}, u32[]{:S(2)}, u32[]{:S(2)}) collective-permute-start(bf16[256,768]{1,0:T(8,128)(2,1)S(1)} %add_convert_fusion), channel_id=1, source_target_pairs={{4,0},{5,1},{6,2},{7,3},{8,4},{9,5},{10,6},{11,7},{12,8},{13,9},{1... | collective-permute-start | bytes 1179656 | tf_op jit(solution)/shard_map/ppermute | solution.py:60
  121.2 1.2 copy-start.2
  121.2 1.5 %copy-start.12 = (f32[1024,256]{0,1:T(8,128)S(1)}, f32[1024,256]{0,1:T(8,128)}, u32[]{:S(2)}) copy-start(f32[1024,256]{0,1:T(8,128)} %copy-done.11) | copy-start | bytes 3145732

commit v2 on v0

v2 whole, which is shorter than its diff:
```python
import jax
import jax.numpy as jnp
from jax import lax
from jax.experimental import pallas as pl
from jax.experimental.pallas import tpu as pltpu
from jax.sharding import PartitionSpec as P

TOK_DEV = 256
STEPS = 4
AXES = ("blk", "group")
ROW = 8
PAD = 16
VMEM_BYTES = 16 * 1024 * 1024
NT = (((1,), (1,)), ((), ()))


def vmem():
    return pl.BlockSpec(memory_space=pltpu.VMEM)


def smem():
    return pl.BlockSpec(memory_space=pltpu.SMEM)


def anywhere():
    return pl.BlockSpec(memory_space=pl.ANY)


def call(kernel, outs, ins, flops, name, args, scratch=()):
    return pl.pallas_call(
        kernel,
        out_shape=outs,
        in_specs=ins,
        out_specs=jax.tree.map(lambda _: vmem(), outs),
        scratch_shapes=scratch,
        compiler_params=pltpu.CompilerParams(vmem_limit_bytes=VMEM_BYTES),
        cost_estimate=pl.CostEstimate(
            flops=flops, bytes_accessed=4 * 1024 * 1024, transcendentals=0
        ),
        name=name,
    )(*args)


def shape(dims, dtype):
    return jax.ShapeDtypeStruct(dims, dtype)


def unit_rows(values):
    as_float = values.astype(jnp.float32)
    inverse = lax.rsqrt(jnp.sum(as_float * as_float, axis=-1, keepdims=True) + 1e-06)
    return as_float * inverse, inverse


def norm_kernel(captions, out):
    out[...] = unit_rows(captions[...])[0].astype(jnp.bfloat16)


def pair_chunk(visiting, image, scale, bias, positive):
    logits = (
        scale * lax.dot_general(visiting, image, NT, preferred_element_type=jnp.float32) + bias
    )
    signed = logits if positive is None else jnp.where(positive, -logits, logits)
    small = jnp.exp(-jnp.abs(signed))
    whole = 1.0 + small
    inverse = 1.0 / whole
    log1p = jnp.log(whole) + (small - (whole - 1.0)) * inverse
    loss = jnp.sum(jnp.maximum(signed, 0.0) + log1p, axis=0, keepdims=True)
    slope = jnp.where(signed >= 0.0, inverse, small * inverse)
    if positive is not None:
        slope = jnp.where(positive, -slope, slope)
    return loss, slope


def first_kernel(images, visiting, pairing, scale, bias, image_bf, loss, slopes, grad, total):
    n, rows = TOK_DEV, image_bf.shape[0]
    held = visiting[...]
    for c in range(rows // n):
        at = slice(c * n, (c + 1) * n)
        image = unit_rows(images[at, :])[0].astype(jnp.bfloat16)
        image_bf[at, :] = image
        positive = pairing[...] == c * n + lax.broadcasted_iota(jnp.int32, (n, n), 1)
        part, slope = pair_chunk(held, image, scale[0], bias[0], positive)
        loss[:, at] = part
        slopes[at, :] = slope.T.astype(jnp.bfloat16)
        term = jnp.dot(slope.astype(jnp.bfloat16), image, preferred_element_type=jnp.float32)
        if c == 0:
            total[...] = term
        elif c < rows // n - 1:
            total[...] += term
        else:
            grad[...] = scale[0] * (total[...] + term)


def next_kernel(place, image_bf, f2, f3, before, scale, bias, loss, slopes, grad, held_out, total):
    n, rows = TOK_DEV, image_bf.shape[0]
    held = jnp.where(place[0] == 2, f2[...], f3[...])
    held_out[...] = held
    for c in range(rows // n):
        at = slice(c * n, (c + 1) * n)
        image = image_bf[at, :]
        part, slope = pair_chunk(held, image, scale[0], bias[0], None)
        loss[:, at] = before[:, at] + part
        slopes[at, :] = slope.T.astype(jnp.bfloat16)
        term = jnp.dot(slope.astype(jnp.bfloat16), image, preferred_element_type=jnp.float32)
        if c == 0:
            total[...] = term
        elif c < rows // n - 1:
            total[...] += term
        else:
            grad[...] = (scale[0] * (total[...] + term)).astype(grad.dtype)


def last_kernel(
    lane, place, scale, bias, image_bf, v0, f1, f2, vc, y1, y2, f5, before, s0_in, sc_in,
    across, near, far, own, grad_a, grad_b, to_swap,
    s0, sa, sb, sc, va, vb, total_a, total_b, loss, sems,
):
    n, rows, g = TOK_DEV, image_bf.shape[0], lane[0]
    copies = [pltpu.make_async_copy(s0_in, s0, sems.at[0]), pltpu.make_async_copy(sc_in, sc, sems.at[1])]
    for copy in copies:
        copy.start()
    first, second, third = place[0] == 0, place[0] == 1, place[0] == 2
    for held, choices in (
        (va, ((first, y1), (~first, f1))),
        (vb, ((first, f5), (second, y1), (third, y2), (place[0] > 2, f2))),
    ):
        for chosen, source in choices:

            @pl.when(chosen)
            def _():
                held[...] = source[...]

    for c in range(rows // n):
        at = slice(c * n, (c + 1) * n)
        image = image_bf[at, :]
        sums = before[:, at]
        for v, s, total in ((va, sa, total_a), (vb, sb, total_b)):
            part, slope = pair_chunk(v[...], image, scale[0], bias[0], None)
            sums = sums + part
            s[at, :] = slope.T.astype(jnp.bfloat16)
            term = jnp.dot(slope.astype(jnp.bfloat16), image, preferred_element_type=jnp.float32)
            if c == 0:
                total[...] = term
            else:
                total[...] += term
        loss[:, at] = sums
    grad_a[...] = (scale[0] * total_a[...]).astype(jnp.bfloat16)
    grad_b[...] = (scale[0] * total_b[...]).astype(jnp.bfloat16)
    to_swap[...] = jnp.where(first, grad_a[...], grad_b[...])
    for copy in copies:
        copy.wait()
    for out, index in ((across, 3 - g), (far, g ^ 2), (near, g ^ 1), (own, g)):
        at = pl.ds(pl.multiple_of(index * n, n), n)
        total = None
        for s, v in ((s0, v0), (sa, va), (sb, vb), (sc, vc)):
            term = jnp.dot(s[at, :], v[...], preferred_element_type=jnp.float32)
            total = term if total is None else total + term
        out[:n, :] = (scale[0] * total).astype(out.dtype)
        sums = loss[:, at]
        high = sums.astype(jnp.bfloat16).astype(jnp.float32)
        row = lax.broadcasted_iota(jnp.int32, (PAD, n), 0)
        tail = jnp.where(row == 0, high, jnp.where(row == 1, sums - high, 0.0))
        out[n:, :n] = tail.astype(out.dtype)
        out[n:, n:] = jnp.zeros((PAD, out.shape[1] - n), out.dtype)


def back_kernel(place, grad_a, grad_b, grad_c, handed_one, handed_two, by_one, by_two, by_three):
    third = place[0] == 2
    gc = grad_c[...].astype(jnp.float32)
    handed = handed_one[...].astype(jnp.float32) + handed_two[...].astype(jnp.float32)
    by_three[...] = (jnp.where(third, 0.0, gc) + handed).astype(jnp.bfloat16)
    by_two[...] = jnp.where(third, grad_c[...], grad_b[...])
    by_one[...] = grad_a[...]


def final_kernel(values, upstream, grad):
    unit, inverse = unit_rows(values)
    grad[...] = inverse * (upstream - unit * jnp.sum(unit * upstream, axis=-1, keepdims=True))


def image_final_kernel(lane, images, own, far, across, near, grad, loss_rows, values, sem):
    n = TOK_DEV
    at = pl.ds(pl.multiple_of(lane[0] * n, n), n)
    copy = pltpu.make_async_copy(images.at[at], values, sem)
    copy.start()
    parts = (own, far, across, near)
    sums = sum(p[n:, :n].astype(jnp.float32) for p in parts)
    loss_rows[...] = jnp.sum(sums, axis=0, keepdims=True) / (STEPS * TOK_DEV)
    copy.wait()
    upstream = sum(p[:n, :].astype(jnp.float32) for p in parts)
    final_kernel(values[...], upstream, grad)


def caption_final_kernel(captions, own, r3, r2, r1, grad):
    upstream = own[...] + sum(r[...].astype(jnp.float32) for r in (r1, r2, r3))
    final_kernel(captions[...], upstream, grad)


def routes(n_blk, n_group):
    def at(b, g):
        return (b % n_blk) * n_group + g

    def inside(pairs):
        return [
            (at(b + s, g), at(b + t, g))
            for b in range(0, n_blk, ROW)
            for g in range(n_group)
            for s, t in pairs
        ]

    def shift(distance):
        return inside([(s, s + distance) for s in range(ROW - distance)])

    def crossing(pairs):
        return [
            (at(b + s, g), at(b + ROW + t, n_group - 1 - g))
            for b in range(0, n_blk, ROW)
            for g in range(n_group)
            for s, t in pairs
        ]

    forward = [
        shift(3) + crossing([(ROW - 1, 1), (ROW - 2, 0)]),
        crossing([(ROW - 3, 0)]),
        shift(1),
        shift(2),
    ]
    back = [
        shift(1),
        shift(2),
        shift(3) + crossing([(ROW - 1, 1), (ROW - 2, 0), (ROW - 3, 2)]),
    ]
    return forward, back, inside([(0, 1), (1, 0)]), inside([(1, 2)]), inside([(2, 1), (0, 2)])


def body(images, captions, pairing, logit_scale, logit_bias):
    n_blk, n_group = lax.axis_size("blk"), lax.axis_size("group")
    forward, back, swap, pass_on, pass_back = routes(n_blk, n_group)
    lane = jnp.full((1,), lax.axis_index("group"), jnp.int32)
    place = jnp.full((1,), lax.axis_index("blk") % ROW, jnp.int32)
    n, width = captions.shape
    rows = images.shape[0]
    flops = 2 * rows * n * width

    def send(block, route):
        return lax.ppermute(block, AXES, route)

    def send_back(block, route):
        return lax.ppermute(block, AXES, [(t, s) for s, t in route])

    def within(block, pairs):
        return lax.ppermute(
            block, AXES, [(b * n_group + s, b * n_group + t) for b in range(n_blk) for s, t in pairs]
        )

    wide, short = jnp.float32, jnp.bfloat16
    slopes = shape((rows, n), short)
    block = shape((n, width), short)
    v0 = call(norm_kernel, block, [vmem()], 1000, "caption_unit", (captions,))
    f3, f5, f1, f2 = [send(v0, route) for route in forward]
    image_bf, loss, s0, g0 = call(
        first_kernel,
        (shape((rows, width), short), shape((1, rows), wide), slopes, shape((n, width), wide)),
        [vmem(), vmem(), vmem(), smem(), smem()],
        2 * flops,
        "first_pairs",
        (images, v0, pairing.reshape(n, 1), logit_scale, logit_bias),
        [pltpu.VMEM((n, width), wide)],
    )
    f3, loss = lax.optimization_barrier((f3, loss))
    y1 = send(f3, swap)
    y2 = send(f3, pass_on)
    loss, sc, gc, vc = call(
        next_kernel,
        (shape((1, rows), wide), slopes, block, block),
        [smem()] + [vmem()] * 4 + [smem(), smem()],
        2 * flops,
        "next_pairs",
        (place, image_bf, f2, f3, loss, logit_scale, logit_bias),
        [pltpu.VMEM((n, width), wide)],
    )
    share = shape((n + PAD, width), short)
    across, near, far, own, ga, gb, to_swap = call(
        last_kernel,
        (share, share, share, shape((n + PAD, width), wide), block, block, block),
        [smem()] * 4 + [vmem()] * 9 + [anywhere()] * 2,
        8 * flops,
        "last_pairs",
        (lane, place, logit_scale, logit_bias, image_bf, v0, f1, f2, vc, y1, y2, f5, loss, s0, sc),
        [pltpu.VMEM((rows, n), short)] * 4
        + [pltpu.VMEM((n, width), short)] * 2
        + [pltpu.VMEM((n, width), wide)] * 2
        + [pltpu.VMEM((1, rows), wide), pltpu.SemaphoreType.DMA((2,))],
    )
    y1 = send(to_swap, swap)
    y2 = send(gb, pass_back)
    far = within(far, [(0, 2), (1, 3), (2, 0), (3, 1)])
    across = within(across, [(0, 3), (1, 2), (2, 1), (3, 0)])
    near = within(near, [(0, 1), (1, 0), (2, 3), (3, 2)])
    ga, gb, gc = call(
        back_kernel,
        (block,) * 3,
        [smem()] + [vmem()] * 5,
        1000,
        "back_sums",
        (place, ga, gb, gc, y1, y2),
    )
    r3 = send_back(gc, back[2])
    r2 = send_back(gb, back[1])
    r1 = send_back(ga, back[0])
    image_grad, loss_rows = call(
        image_final_kernel,
        (shape((n, width), wide), shape((1, n), wide)),
        [smem(), anywhere()] + [vmem()] * 4,
        1000,
        "image_final",
        (lane, images, own, far, across, near),
        [pltpu.VMEM((n, width), short), pltpu.SemaphoreType.DMA],
    )
    caption_grad = call(
        caption_final_kernel,
        shape((n, width), wide),
        [vmem()] * 5,
        1000,
        "caption_final",
        (captions, g0, r3, r2, r1),
    )
    return (image_grad, caption_grad, loss_rows.reshape(n))


def solution(mesh):
    in_specs = (P("blk", None), P(("blk", "group"), None), P("blk", "group"), P(), P())
    out_specs = (P(("blk", "group"), None), P(("blk", "group"), None), P(("blk", "group")))
    return jax.shard_map(body, mesh=mesh, in_specs=in_specs, out_specs=out_specs, check_vma=False)
```

time: 239 us -> 102 us (0.43)
  the two profiles are of different devices: /device:TPU:397 before, /device:TPU:1 now
where the time goes in v2:
time: 102 us; the launch traced here: 101 us
  waiting for transfers between devices  43.4 us (43%)
  starting transfers between devices  35.7 us (35%)
  Pallas kernels  13.4 us (13%)
  local copies, waits for them, and re-layouts  6.59 us (6%)
  between operations  2.24 us (2%)
    ppermute x3, waiting for transfers between devices, within(): lax.ppermute(block, AXES, [(b * n_group + s, b * n_group + t) for b in ra...  23.4 us
    ppermute x8, waiting for transfers between devices, send(): return lax.ppermute(block, AXES, route)  20 us
    ppermute x8, starting transfers between devices, send(): return lax.ppermute(block, AXES, route)  19.5 us
    pallas_call x7, Pallas kernels, call(): pl.pallas_call(kernel, out_shape=outs, in_specs=ins, out_specs=jax.tree.m...  13.4 us
    ppermute x3, starting transfers between devices, within(): lax.ppermute(block, AXES, [(b * n_group + s, b * n_group + t) for b in ra...  10.3 us
    ppermute x3, starting transfers between devices, send_back(): return lax.ppermute(block, AXES, [(t, s) for s, t in route])  5.88 us
    unnamed x18, local copies, waits for them, and re-layouts  5.78 us
  transfers between devices with their start and end apart: 14, of which 4 were waited for; matrix products, arithmetic and copies ran while one was open for 1% of the time, Pallas kernels for 5%

profile of v2, /device:TPU:1, one launch (start us, length us, event | category | flops | bytes accessed | tf_op | source)
XLA Modules:
  0.0 101.4 jit_solution(8054497069156036909)
XLA Ops:
  0.6 0.0 copy-start
  0.6 1.0 copy-done
  1.6 0.2 caption_unit.1.visiting.v0
  1.8 6.0 %collective-permute-start.2 = (bf16[256,768]{1,0:T(8,128)(2,1)S(1)}, bf16[256,768]{1,0:T(8,128)(2,1)S(1)}, u32[]{:S(2)}, u32[]{:S(2)}) collective-permute-start(bf16[256,768]{1,0:T(8,128)(2,1)S(1)} %caption_unit.1.visiting.v0), channel_id=1, source_target_pairs={{0,12},{4,16},{8,20},{12,24},{16,28},{1,13},{5,17},{9,21},{13,25},... | collective-permute-start | bytes 1179656 | tf_op jit(solution)/shard_map/ppermute | solution.py:246
  7.8 0.7 collective-permute-start.5
  8.5 2.2 %collective-permute-start.1 = (bf16[256,768]{1,0:T(8,128)(2,1)S(1)}, bf16[256,768]{1,0:T(8,128)(2,1)S(1)}, u32[]{:S(2)}, u32[]{:S(2)}) collective-permute-start(bf16[256,768]{1,0:T(8,128)(2,1)S(1)} %caption_unit.1.visiting.v0), channel_id=1, source_target_pairs={{0,8},{4,12},{8,16},{12,20},{16,24},{20,28},{1,9},{5,13},{9,17},{1... | collective-permute-start | bytes 1179656 | tf_op jit(solution)/shard_map/ppermute | solution.py:246
  10.8 2.2 %collective-permute-start = (bf16[256,768]{1,0:T(8,128)(2,1)S(1)}, bf16[256,768]{1,0:T(8,128)(2,1)S(1)}, u32[]{:S(2)}, u32[]{:S(2)}) collective-permute-start(bf16[256,768]{1,0:T(8,128)(2,1)S(1)} %caption_unit.1.visiting.v0), channel_id=1, source_target_pairs={{0,4},{4,8},{8,12},{12,16},{16,20},{20,24},{24,28},{1,5},{5,9},{9,... | collective-permute-start | bytes 1179656 | tf_op jit(solution)/shard_map/ppermute | solution.py:246
  14.3 0.8 copy.8.pairing
  15.1 0.0 copy-start.2
  15.1 1.4 %copy-done.2 = bf16[1024,768]{1,0:T(8,128)(2,1)S(1)} copy-done((bf16[1024,768]{1,0:T(8,128)(2,1)S(1)}, bf16[1024,768]{1,0:T(8,128)(2,1)}, u32[]{:S(2)}) %copy-start.2) | copy-done | bytes 1572888
  16.5 2.2 %first_pairs.1 = (bf16[1024,768]{1,0:T(8,128)(2,1)S(1)}, f32[1,1024]{1,0:T(1,128)S(1)}, bf16[1024,256]{1,0:T(8,128)(2,1)S(1)}, f32[256,768]{1,0:T(8,128)S(1)}) custom-call(bf16[1024,768]{1,0:T(8,128)(2,1)S(1)} %copy-done.2, bf16[256,768]{1,0:T(8,128)(2,1)S(1)} %caption_unit.1.visiting.v0, s32[256,1]{1,0:T(8,128)S(1)} %copy.8.pairing, f32[1]{0:T(128)S(6)} %copy.9.scale, ...), custom_call_target="tpu_custom_call" | custom-call | flops 805306368 | bytes 4194304 | tf_op jit(solution)/shard_map/first_pairs/pallas_call | solution.py:30
  18.7 0.0 copy-start.4
  18.7 1.2 %copy-done.4 = bf16[1024,768]{1,0:T(8,128)(2,1)} copy-done((bf16[1024,768]{1,0:T(8,128)(2,1)}, bf16[1024,768]{1,0:T(8,128)(2,1)S(1)}, u32[]{:S(2)}) %copy-start.4) | copy-done | bytes 1572888
  19.8 0.8 copy-done.7
  20.6 16.4 %collective-permute-done.2.f3 = bf16[256,768]{1,0:T(8,128)(2,1)S(1)} collective-permute-done((bf16[256,768]{1,0:T(8,128)(2,1)S(1)}, bf16[256,768]{1,0:T(8,128)(2,1)S(1)}, u32[]{:S(2)}, u32[]{:S(2)}) %collective-permute-start.2) | collective-permute-done | bytes 393248 | tf_op jit(solution)/shard_map/ppermute | solution.py:246
  37.0 1.3 %collective-permute-start.4 = (bf16[256,768]{1,0:T(8,128)(2,1)S(1)}, bf16[256,768]{1,0:T(8,128)(2,1)S(1)}, u32[]{:S(2)}, u32[]{:S(2)}) collective-permute-start(bf16[256,768]{1,0:T(8,128)(2,1)S(1)} %collective-permute-done.2.f3), channel_id=1, source_target_pairs={{4,8},{5,9},{6,10},{7,11},{36,40},{37,41},{38,42},{39,43},{68,72},... | collective-permute-start | bytes 1179656 | tf_op jit(solution)/shard_map/ppermute | solution.py:246
  38.4 3.6 %collective-permute-start.3 = (bf16[256,768]{1,0:T(8,128)(2,1)S(1)}, bf16[256,768]{1,0:T(8,128)(2,1)}, u32[]{:S(2)}, u32[]{:S(2)}) collective-permute-start(bf16[256,768]{1,0:T(8,128)(2,1)S(1)} %collective-permute-done.2.f3), channel_id=1, source_target_pairs={{0,4},{4,0},{1,5},{5,1},{2,6},{6,2},{3,7},{7,3},{32,36},{36,32},{3... | collective-permute-start | bytes 1179656 | tf_op jit(solution)/shard_map/ppermute | solution.py:246
  42.0 0.0 collective-permute-done.1.f2
  42.0 0.0 copy-start.5
  42.0 1.4 %copy-done.5 = bf16[1024,768]{1,0:T(8,128)(2,1)S(1)} copy-done((bf16[1024,768]{1,0:T(8,128)(2,1)S(1)}, bf16[1024,768]{1,0:T(8,128)(2,1)}, u32[]{:S(2)}) %copy-start.5) | copy-done | bytes 1572888
  43.4 1.6 %next_pairs.1 = (f32[1,1024]{1,0:T(1,128)S(1)}, bf16[1024,256]{1,0:T(8,128)(2,1)S(1)}, bf16[256,768]{1,0:T(8,128)(2,1)S(1)}, bf16[256,768]{1,0:T(8,128)(2,1)S(1)}) custom-call(s32[1]{0:T(128)} %bitcast.1.place, bf16[1024,768]{1,0:T(8,128)(2,1)S(1)} %copy-done.5, bf16[256,768]{1,0:T(8,128)(2,1)S(1)} %collective-permute-done.1.f2, ...), custom_call_target="tpu_custom_call" | custom-call | flops 805306368 | bytes 4194304 | tf_op jit(solution)/shard_map/next_pairs/pallas_call | solution.py:30
  45.0 0.0 collective-permute-done.5.f5
  45.1 0.0 collective-permute-done.f1
  45.1 0.0 collective-permute-done.4.y2
  45.1 0.0 collective-permute-done.3.y1
  45.1 0.0 copy-done.6
  45.1 6.4 %last_pairs.1 = (bf16[272,768]{1,0:T(8,128)(2,1)S(1)}, bf16[272,768]{1,0:T(8,128)(2,1)S(1)}, bf16[272,768]{1,0:T(8,128)(2,1)S(1)}, f32[272,768]{1,0:T(8,128)S(1)...) custom-call(s32[1]{0:T(128)} %bitcast.lane, s32[1]{0:T(128)} %bitcast.1.place, ...), custom_call_target="tpu_custom_call" | custom-call | flops 3221225472 | bytes 4194304 | tf_op jit(solution)/shard_map/last_pairs/pallas_call | solution.py:30
  51.5 0.0 copy-start.3
  51.6 5.8 %collective-permute-start.6 = (bf16[272,768]{1,0:T(8,128)(2,1)S(1)}, bf16[272,768]{1,0:T(8,128)(2,1)S(1)}, u32[]{:S(2)}, u32[]{:S(2)}) collective-permute-start(bf16[272,768]{1,0:T(8,128)(2,1)S(1)} %get-tuple-element.34), channel_id=1, source_target_pairs={{0,2},{1,3},{2,0},{3,1},{4,6},{5,7},{6,4},{7,5},{8,10},{9,11},{10,... | collective-permute-start | bytes 1253384 | tf_op jit(solution)/shard_map/ppermute | solution.py:252
  57.4 2.2 %collective-permute-start.9 = (bf16[256,768]{1,0:T(8,128)(2,1)S(1)}, bf16[256,768]{1,0:T(8,128)(2,1)S(1)}, u32[]{:S(2)}, u32[]{:S(2)}) collective-permute-start(bf16[256,768]{1,0:T(8,128)(2,1)S(1)} %get-tuple-element.42), channel_id=1, source_target_pairs={{0,4},{4,0},{1,5},{5,1},{2,6},{6,2},{3,7},{7,3},{32,36},{36,32},{3... | collective-permute-start | bytes 1179656 | tf_op jit(solution)/shard_map/ppermute | solution.py:246
  59.6 1.3 %collective-permute-start.10 = (bf16[256,768]{1,0:T(8,128)(2,1)S(1)}, bf16[256,768]{1,0:T(8,128)(2,1)S(1)}, u32[]{:S(2)}, u32[]{:S(2)}) collective-permute-start(bf16[256,768]{1,0:T(8,128)(2,1)S(1)} %get-tuple-element.40.grad_b), channel_id=1, source_target_pairs={{8,4},{0,8},{9,5},{1,9},{10,6},{2,10},{11,7},{3,11},{40,36},{32,40... | collective-permute-start | bytes 1179656 | tf_op jit(solution)/shard_map/ppermute | solution.py:246
  60.9 2.5 %collective-permute-start.7 = (bf16[272,768]{1,0:T(8,128)(2,1)S(1)}, bf16[272,768]{1,0:T(8,128)(2,1)S(1)}, u32[]{:S(2)}, u32[]{:S(2)}) collective-permute-start(bf16[272,768]{1,0:T(8,128)(2,1)S(1)} %get-tuple-element.35), channel_id=1, source_target_pairs={{0,3},{1,2},{2,1},{3,0},{4,7},{5,6},{6,5},{7,4},{8,11},{9,10},{10,... | collective-permute-start | bytes 1253384 | tf_op jit(solution)/shard_map/ppermute | solution.py:252
  63.4 1.9 %collective-permute-start.8 = (bf16[272,768]{1,0:T(8,128)(2,1)S(1)}, bf16[272,768]{1,0:T(8,128)(2,1)S(1)}, u32[]{:S(2)}, u32[]{:S(2)}) collective-permute-start(bf16[272,768]{1,0:T(8,128)(2,1)S(1)} %get-tuple-element.36), channel_id=1, source_target_pairs={{0,1},{1,0},{2,3},{3,2},{4,5},{5,4},{6,7},{7,6},{8,9},{9,8},{10,11... | collective-permute-start | bytes 1253384 | tf_op jit(solution)/shard_map/ppermute | solution.py:252
  65.4 0.0 collective-permute-done.9.handed_one
  65.4 3.6 %collective-permute-done.10.handed_two = bf16[256,768]{1,0:T(8,128)(2,1)S(1)} collective-permute-done((bf16[256,768]{1,0:T(8,128)(2,1)S(1)}, bf16[256,768]{1,0:T(8,128)(2,1)S(1)}, u32[]{:S(2)}, u32[]{:S(2)}) %collective-permute-start.10) | collective-permute-done | bytes 393248 | tf_op jit(solution)/shard_map/ppermute | solution.py:246
  69.0 0.2 back_sums.1
  69.2 1.9 %collective-permute-start.11 = (bf16[256,768]{1,0:T(8,128)(2,1)S(1)}, bf16[256,768]{1,0:T(8,128)(2,1)S(1)}, u32[]{:S(2)}, u32[]{:S(2)}) collective-permute-start(bf16[256,768]{1,0:T(8,128)(2,1)S(1)} %get-tuple-element.43), channel_id=1, source_target_pairs={{12,0},{16,4},{20,8},{24,12},{28,16},{13,1},{17,5},{21,9},{25,13},... | collective-permute-start | bytes 1179656 | tf_op jit(solution)/shard_map/ppermute | solution.py:249
  71.1 1.3 %collective-permute-start.12 = (bf16[256,768]{1,0:T(8,128)(2,1)S(1)}, bf16[256,768]{1,0:T(8,128)(2,1)S(1)}, u32[]{:S(2)}, u32[]{:S(2)}) collective-permute-start(bf16[256,768]{1,0:T(8,128)(2,1)S(1)} %get-tuple-element.44), channel_id=1, source_target_pairs={{8,0},{12,4},{16,8},{20,12},{24,16},{28,20},{9,1},{13,5},{17,9},{2... | collective-permute-start | bytes 1179656 | tf_op jit(solution)/shard_map/ppermute | solution.py:249
  72.4 17.1 %collective-permute-done.6.far = bf16[272,768]{1,0:T(8,128)(2,1)S(1)} collective-permute-done((bf16[272,768]{1,0:T(8,128)(2,1)S(1)}, bf16[272,768]{1,0:T(8,128)(2,1)S(1)}, u32[]{:S(2)}, u32[]{:S(2)}) %collective-permute-start.6) | collective-permute-done | bytes 417824 | tf_op jit(solution)/shard_map/ppermute | solution.py:252
  89.5 2.7 %collective-permute-start.13 = (bf16[256,768]{1,0:T(8,128)(2,1)S(1)}, bf16[256,768]{1,0:T(8,128)(2,1)S(1)}, u32[]{:S(2)}, u32[]{:S(2)}) collective-permute-start(bf16[256,768]{1,0:T(8,128)(2,1)S(1)} %get-tuple-element.45), channel_id=1, source_target_pairs={{4,0},{8,4},{12,8},{16,12},{20,16},{24,20},{28,24},{5,1},{9,5},{13... | collective-permute-start | bytes 1179656 | tf_op jit(solution)/shard_map/ppermute | solution.py:249
  92.2 0.0 collective-permute-done.7.across
  92.2 6.3 %collective-permute-done.8.near = bf16[272,768]{1,0:T(8,128)(2,1)S(1)} collective-permute-done((bf16[272,768]{1,0:T(8,128)(2,1)S(1)}, bf16[272,768]{1,0:T(8,128)(2,1)S(1)}, u32[]{:S(2)}, u32[]{:S(2)}) %collective-permute-start.8) | collective-permute-done | bytes 417824 | tf_op jit(solution)/shard_map/ppermute | solution.py:252
  98.5 1.5 %image_final.1 = (f32[256,768]{1,0:T(8,128)}, f32[1,256]{1,0:T(1,128)}) custom-call(s32[1]{0:T(128)} %bitcast.lane, bf16[1024,768]{1,0:T(8,128)(2,1)S(1)} %copy-done.3, f32[272,768]{1,0:T(8,128)S(1)} %get-tuple-element.33.own, bf16[272,768]{1,0:T(8,128)(2,1)S(1)} %collective-permute-done.6.far, bf16[272,768]{1,0:T(8,128)(2,1)S(1)} %collective-permute-done.7.across, ...), custom_call_target="tpu_custom_call" | custom-call | flops 1000 | bytes 4194304 | tf_op jit(solution)/shard_map/image_final/pallas_call | solution.py:30
  100.0 0.0 collective-permute-done.11.r3
  100.1 0.0 collective-permute-done.12.r2
  100.1 0.0 collective-permute-done.13.r1
  100.1 0.0 copy-done.1
  100.1 1.3 %caption_final.1 = f32[256,768]{1,0:T(8,128)} custom-call(bf16[256,768]{1,0:T(8,128)(2,1)S(1)} %copy-done.1, f32[256,768]{1,0:T(8,128)S(1)} %get-tuple-element.38.own, bf16[256,768]{1,0:T(8,128)(2,1)S(1)} %collective-permute-done.11.r3, bf16[256,768]{1,0:T(8,128)(2,1)S(1)} %collective-permute-done.12.r2, bf16[256,768]{1,0:T(8,128)(2,1)S(1)} %collective-permute-done.13.r1), custom_call_target="tpu_custom_call" | custom-call | flops 1000 | bytes 4194304 | tf_op jit(solution)/shard_map/caption_final/pallas_call | solution.py:30
  (6 shorter events, 0.0 us)
Async XLA Ops:
  0.6 1.0 copy-start
  1.8 35.3 %collective-permute-start.2 = (bf16[256,768]{1,0:T(8,128)(2,1)S(1)}, bf16[256,768]{1,0:T(8,128)(2,1)S(1)}, u32[]{:S(2)}, u32[]{:S(2)}) collective-permute-start(bf16[256,768]{1,0:T(8,128)(2,1)S(1)} %caption_unit.1.visiting.v0), channel_id=1, source_target_pairs={{0,12},{4,16},{8,20},{12,24},{16,28},{1,13},{5,17},{9,21},{13,25},... | collective-permute-start | bytes 1179656 | tf_op jit(solution)/shard_map/ppermute | solution.py:246
  7.8 37.2 %collective-permute-start.5 = (bf16[256,768]{1,0:T(8,128)(2,1)S(1)}, bf16[256,768]{1,0:T(8,128)(2,1)S(1)}, u32[]{:S(2)}, u32[]{:S(2)}) collective-permute-start(bf16[256,768]{1,0:T(8,128)(2,1)S(1)} %caption_unit.1.visiting.v0), channel_id=1, source_target_pairs={{20,35},{21,34},{22,33},{23,32},{52,67},{53,66},{54,65},{55,64},{8... | collective-permute-start | bytes 1179656 | tf_op jit(solution)/shard_map/ppermute | solution.py:246
  8.5 33.5 %collective-permute-start.1 = (bf16[256,768]{1,0:T(8,128)(2,1)S(1)}, bf16[256,768]{1,0:T(8,128)(2,1)S(1)}, u32[]{:S(2)}, u32[]{:S(2)}) collective-permute-start(bf16[256,768]{1,0:T(8,128)(2,1)S(1)} %caption_unit.1.visiting.v0), channel_id=1, source_target_pairs={{0,8},{4,12},{8,16},{12,20},{16,24},{20,28},{1,9},{5,13},{9,17},{1... | collective-permute-start | bytes 1179656 | tf_op jit(solution)/shard_map/ppermute | solution.py:246
  10.8 34.3 %collective-permute-start = (bf16[256,768]{1,0:T(8,128)(2,1)S(1)}, bf16[256,768]{1,0:T(8,128)(2,1)S(1)}, u32[]{:S(2)}, u32[]{:S(2)}) collective-permute-start(bf16[256,768]{1,0:T(8,128)(2,1)S(1)} %caption_unit.1.visiting.v0), channel_id=1, source_target_pairs={{0,4},{4,8},{8,12},{12,16},{16,20},{20,24},{24,28},{1,5},{5,9},{9,... | collective-permute-start | bytes 1179656 | tf_op jit(solution)/shard_map/ppermute | solution.py:246
  15.1 1.4 %copy-start.2 = (bf16[1024,768]{1,0:T(8,128)(2,1)S(1)}, bf16[1024,768]{1,0:T(8,128)(2,1)}, u32[]{:S(2)}) copy-start(bf16[1024,768]{1,0:T(8,128)(2,1)} %images.3) | copy-start | bytes 4718596
  18.7 1.2 %copy-start.4 = (bf16[1024,768]{1,0:T(8,128)(2,1)}, bf16[1024,768]{1,0:T(8,128)(2,1)S(1)}, u32[]{:S(2)}) copy-start(bf16[1024,768]{1,0:T(8,128)(2,1)S(1)} %get-tuple-element.25.image_bf) | copy-start | bytes 4718596
  19.8 0.8 copy-start.7
  37.0 8.0 %collective-permute-start.4 = (bf16[256,768]{1,0:T(8,128)(2,1)S(1)}, bf16[256,768]{1,0:T(8,128)(2,1)S(1)}, u32[]{:S(2)}, u32[]{:S(2)}) collective-permute-start(bf16[256,768]{1,0:T(8,128)(2,1)S(1)} %collective-permute-done.2.f3), channel_id=1, source_target_pairs={{4,8},{5,9},{6,10},{7,11},{36,40},{37,41},{38,42},{39,43},{68,72},... | collective-permute-start | bytes 1179656 | tf_op jit(solution)/shard_map/ppermute | solution.py:246
  38.4 6.7 %collective-permute-start.3 = (bf16[256,768]{1,0:T(8,128)(2,1)S(1)}, bf16[256,768]{1,0:T(8,128)(2,1)}, u32[]{:S(2)}, u32[]{:S(2)}) collective-permute-start(bf16[256,768]{1,0:T(8,128)(2,1)S(1)} %collective-permute-done.2.f3), channel_id=1, source_target_pairs={{0,4},{4,0},{1,5},{5,1},{2,6},{6,2},{3,7},{7,3},{32,36},{36,32},{3... | collective-permute-start | bytes 1179656 | tf_op jit(solution)/shard_map/ppermute | solution.py:246
  42.0 1.4 %copy-start.5 = (bf16[1024,768]{1,0:T(8,128)(2,1)S(1)}, bf16[1024,768]{1,0:T(8,128)(2,1)}, u32[]{:S(2)}) copy-start(bf16[1024,768]{1,0:T(8,128)(2,1)} %copy-done.4) | copy-start | bytes 4718596
  43.4 1.7 %copy-start.6 = (bf16[1024,768]{1,0:T(8,128)(2,1)S(1)}, bf16[1024,768]{1,0:T(8,128)(2,1)}, u32[]{:S(2)}) copy-start(bf16[1024,768]{1,0:T(8,128)(2,1)} %copy-done.4) | copy-start | bytes 4718596
  43.4 1.7 %copy-start.8 = (bf16[1024,256]{1,0:T(8,128)(2,1)S(1)}, bf16[1024,256]{1,0:T(8,128)(2,1)}, u32[]{:S(2)}) copy-start(bf16[1024,256]{1,0:T(8,128)(2,1)} %copy-done.7) | copy-start | bytes 1572868
  51.5 47.0 %copy-start.3 = (bf16[1024,768]{1,0:T(8,128)(2,1)S(1)}, bf16[1024,768]{1,0:T(8,128)(2,1)}, u32[]{:S(2)}) copy-start(bf16[1024,768]{1,0:T(8,128)(2,1)} %images.3) | copy-start | bytes 4718596
  51.6 38.0 %collective-permute-start.6 = (bf16[272,768]{1,0:T(8,128)(2,1)S(1)}, bf16[272,768]{1,0:T(8,128)(2,1)S(1)}, u32[]{:S(2)}, u32[]{:S(2)}) collective-permute-start(bf16[272,768]{1,0:T(8,128)(2,1)S(1)} %get-tuple-element.34), channel_id=1, source_target_pairs={{0,2},{1,3},{2,0},{3,1},{4,6},{5,7},{6,4},{7,5},{8,10},{9,11},{10,... | collective-permute-start | bytes 1253384 | tf_op jit(solution)/shard_map/ppermute | solution.py:252
  57.4 8.0 %collective-permute-start.9 = (bf16[256,768]{1,0:T(8,128)(2,1)S(1)}, bf16[256,768]{1,0:T(8,128)(2,1)S(1)}, u32[]{:S(2)}, u32[]{:S(2)}) collective-permute-start(bf16[256,768]{1,0:T(8,128)(2,1)S(1)} %get-tuple-element.42), channel_id=1, source_target_pairs={{0,4},{4,0},{1,5},{5,1},{2,6},{6,2},{3,7},{7,3},{32,36},{36,32},{3... | collective-permute-start | bytes 1179656 | tf_op jit(solution)/shard_map/ppermute | solution.py:246
  59.6 9.4 %collective-permute-start.10 = (bf16[256,768]{1,0:T(8,128)(2,1)S(1)}, bf16[256,768]{1,0:T(8,128)(2,1)S(1)}, u32[]{:S(2)}, u32[]{:S(2)}) collective-permute-start(bf16[256,768]{1,0:T(8,128)(2,1)S(1)} %get-tuple-element.40.grad_b), channel_id=1, source_target_pairs={{8,4},{0,8},{9,5},{1,9},{10,6},{2,10},{11,7},{3,11},{40,36},{32,40... | collective-permute-start | bytes 1179656 | tf_op jit(solution)/shard_map/ppermute | solution.py:246
  60.9 31.3 %collective-permute-start.7 = (bf16[272,768]{1,0:T(8,128)(2,1)S(1)}, bf16[272,768]{1,0:T(8,128)(2,1)S(1)}, u32[]{:S(2)}, u32[]{:S(2)}) collective-permute-start(bf16[272,768]{1,0:T(8,128)(2,1)S(1)} %get-tuple-element.35), channel_id=1, source_target_pairs={{0,3},{1,2},{2,1},{3,0},{4,7},{5,6},{6,5},{7,4},{8,11},{9,10},{10,... | collective-permute-start | bytes 1253384 | tf_op jit(solution)/shard_map/ppermute | solution.py:252
  63.4 35.1 %collective-permute-start.8 = (bf16[272,768]{1,0:T(8,128)(2,1)S(1)}, bf16[272,768]{1,0:T(8,128)(2,1)S(1)}, u32[]{:S(2)}, u32[]{:S(2)}) collective-permute-start(bf16[272,768]{1,0:T(8,128)(2,1)S(1)} %get-tuple-element.36), channel_id=1, source_target_pairs={{0,1},{1,0},{2,3},{3,2},{4,5},{5,4},{6,7},{7,6},{8,9},{9,8},{10,11... | collective-permute-start | bytes 1253384 | tf_op jit(solution)/shard_map/ppermute | solution.py:252
  69.2 30.9 %collective-permute-start.11 = (bf16[256,768]{1,0:T(8,128)(2,1)S(1)}, bf16[256,768]{1,0:T(8,128)(2,1)S(1)}, u32[]{:S(2)}, u32[]{:S(2)}) collective-permute-start(bf16[256,768]{1,0:T(8,128)(2,1)S(1)} %get-tuple-element.43), channel_id=1, source_target_pairs={{12,0},{16,4},{20,8},{24,12},{28,16},{13,1},{17,5},{21,9},{25,13},... | collective-permute-start | bytes 1179656 | tf_op jit(solution)/shard_map/ppermute | solution.py:249
  71.1 28.9 %collective-permute-start.12 = (bf16[256,768]{1,0:T(8,128)(2,1)S(1)}, bf16[256,768]{1,0:T(8,128)(2,1)S(1)}, u32[]{:S(2)}, u32[]{:S(2)}) collective-permute-start(bf16[256,768]{1,0:T(8,128)(2,1)S(1)} %get-tuple-element.44), channel_id=1, source_target_pairs={{8,0},{12,4},{16,8},{20,12},{24,16},{28,20},{9,1},{13,5},{17,9},{2... | collective-permute-start | bytes 1179656 | tf_op jit(solution)/shard_map/ppermute | solution.py:249
  89.5 10.6 %collective-permute-start.13 = (bf16[256,768]{1,0:T(8,128)(2,1)S(1)}, bf16[256,768]{1,0:T(8,128)(2,1)S(1)}, u32[]{:S(2)}, u32[]{:S(2)}) collective-permute-start(bf16[256,768]{1,0:T(8,128)(2,1)S(1)} %get-tuple-element.45), channel_id=1, source_target_pairs={{4,0},{8,4},{12,8},{16,12},{20,16},{24,20},{28,24},{5,1},{9,5},{13... | collective-permute-start | bytes 1179656 | tf_op jit(solution)/shard_map/ppermute | solution.py:249
  98.5 1.6 %copy-start.1 = (bf16[256,768]{1,0:T(8,128)(2,1)S(1)}, bf16[256,768]{1,0:T(8,128)(2,1)}, u32[]{:S(2)}) copy-start(bf16[256,768]{1,0:T(8,128)(2,1)} %captions.3) | copy-start | bytes 1179652

commit v3 on v2

--- a/solution.py
+++ b/solution.py
@@ -10,6 +10,7 @@
 AXES = ("blk", "group")
 ROW = 8
 PAD = 16
+NEAR_FLOPS = 1 * 10**9
 VMEM_BYTES = 16 * 1024 * 1024
 NT = (((1,), (1,)), ((), ()))
 
@@ -110,58 +111,87 @@
             grad[...] = (scale[0] * (total[...] + term)).astype(grad.dtype)
 
 
-def last_kernel(
+def write_share(out, total, sums):
+    n = TOK_DEV
+    out[:n, :] = total.astype(out.dtype)
+    high = sums.astype(jnp.bfloat16).astype(jnp.float32)
+    row = lax.broadcasted_iota(jnp.int32, (PAD, n), 0)
+    tail = jnp.where(row == 0, high, jnp.where(row == 1, sums - high, 0.0))
+    out[n:, :n] = tail.astype(out.dtype)
+    out[n:, n:] = jnp.zeros((PAD, out.shape[1] - n), out.dtype)
+
+
+def rows_of(index):
+    return pl.ds(pl.multiple_of(index * TOK_DEV, TOK_DEV), TOK_DEV)
+
+
+def choose(held, choices):
+    for chosen, source in choices:
+
+        @pl.when(chosen)
+        def _():
+            held[...] = source[...]
+
+
+def head_kernel(
     lane, place, scale, bias, image_bf, v0, f1, f2, vc, y1, y2, f5, before, s0_in, sc_in,
-    across, near, far, own, grad_a, grad_b, to_swap,
-    s0, sa, sb, sc, va, vb, total_a, total_b, loss, sems,
+    share, va, vb, slope_a, slope_b, s0, sc, sems,
 ):
-    n, rows, g = TOK_DEV, image_bf.shape[0], lane[0]
-    copies = [pltpu.make_async_copy(s0_in, s0, sems.at[0]), pltpu.make_async_copy(sc_in, sc, sems.at[1])]
+    p, at = place[0], rows_of(3 - lane[0])
+    copies = [
+        pltpu.make_async_copy(s0_in.at[at], s0, sems.at[0]),
+        pltpu.make_async_copy(sc_in.at[at], sc, sems.at[1]),
+    ]
     for copy in copies:
         copy.start()
-    first, second, third = place[0] == 0, place[0] == 1, place[0] == 2
-    for held, choices in (
-        (va, ((first, y1), (~first, f1))),
-        (vb, ((first, f5), (second, y1), (third, y2), (place[0] > 2, f2))),
-    ):
-        for chosen, source in choices:
-
-            @pl.when(chosen)
-            def _():
-                held[...] = source[...]
-
-    for c in range(rows // n):
-        at = slice(c * n, (c + 1) * n)
-        image = image_bf[at, :]
-        sums = before[:, at]
-        for v, s, total in ((va, sa, total_a), (vb, sb, total_b)):
+    choose(va, ((p == 0, y1), (p != 0, f1)))
+    choose(vb, ((p == 0, f5), (p == 1, y1), (p == 2, y2), (p > 2, f2)))
+    image, sums, total = image_bf[at, :], before[:, at], None
+    for v, kept in ((va, slope_a), (vb, slope_b)):
+        part, slope = pair_chunk(v[...], image, scale[0], bias[0], None)
+        sums = sums + part
+        kept[...] = slope.astype(jnp.bfloat16)
+        term = jnp.dot(slope.T.astype(jnp.bfloat16), v[...], preferred_element_type=jnp.float32)
+        total = term if total is None else total + term
+    for copy in copies:
+        copy.wait()
+    for s, v in ((s0, v0), (sc, vc)):
+        total = total + jnp.dot(s[...], v[...], preferred_element_type=jnp.float32)
+    write_share(share, scale[0] * total, sums)
+
+
+def tail_kernel(
+    lane, place, scale, bias, image_bf, v0, va, vb, vc, slope_a, slope_b, before, s0_in, sc_in,
+    far, near, own, grad_a, grad_b, to_swap, s0, sc, total_a, total_b, sems,
+):
+    g = lane[0]
+    copies = [
+        pltpu.make_async_copy(s0_in, s0, sems.at[0]),
+        pltpu.make_async_copy(sc_in, sc, sems.at[1]),
+    ]
+    for copy in copies:
+        copy.start()
+    image = image_bf[rows_of(3 - g), :]
+    total_a[...] = jnp.dot(slope_a[...], image, preferred_element_type=jnp.float32)
+    total_b[...] = jnp.dot(slope_b[...], image, preferred_element_type=jnp.float32)
+    for out, index in ((far, g ^ 2), (near, g ^ 1), (own, g)):
+        at = rows_of(index)
+        image, sums, total = image_bf[at, :], before[:, at], None
+        for v, gained in ((va, total_a), (vb, total_b)):
             part, slope = pair_chunk(v[...], image, scale[0], bias[0], None)
             sums = sums + part
-            s[at, :] = slope.T.astype(jnp.bfloat16)
-            term = jnp.dot(slope.astype(jnp.bfloat16), image, preferred_element_type=jnp.float32)
-            if c == 0:
-                total[...] = term
-            else:
-                total[...] += term
-        loss[:, at] = sums
+            gained[...] += jnp.dot(slope.astype(jnp.bfloat16), image, preferred_element_type=jnp.float32)
+            term = jnp.dot(slope.T.astype(jnp.bfloat16), v[...], preferred_element_type=jnp.float32)
+            total = term if total is None else total + term
+        if out is far:
+            for copy in copies:
+                copy.wait()
+        for s, v in ((s0, v0), (sc, vc)):
+            total = total + jnp.dot(s[at, :], v[...], preferred_element_type=jnp.float32)
+        write_share(out, scale[0] * total, sums)
     grad_a[...] = (scale[0] * total_a[...]).astype(jnp.bfloat16)
     grad_b[...] = (scale[0] * total_b[...]).astype(jnp.bfloat16)
-    to_swap[...] = jnp.where(first, grad_a[...], grad_b[...])
-    for copy in copies:
-        copy.wait()
-    for out, index in ((across, 3 - g), (far, g ^ 2), (near, g ^ 1), (own, g)):
-        at = pl.ds(pl.multiple_of(index * n, n), n)
-        total = None
-        for s, v in ((s0, v0), (sa, va), (sb, vb), (sc, vc)):
-            term = jnp.dot(s[at, :], v[...], preferred_element_type=jnp.float32)
-            total = term if total is None else total + term
-        out[:n, :] = (scale[0] * total).astype(out.dtype)
-        sums = loss[:, at]
-        high = sums.astype(jnp.bfloat16).astype(jnp.float32)
-        row = lax.broadcasted_iota(jnp.int32, (PAD, n), 0)
-        tail = jnp.where(row == 0, high, jnp.where(row == 1, sums - high, 0.0))
-        out[n:, :n] = tail.astype(out.dtype)
-        out[n:, n:] = jnp.zeros((PAD, out.shape[1] - n), out.dtype)
+    to_swap[...] = jnp.where(place[0] == 0, grad_a[...], grad_b[...])
 
 
 def back_kernel(place, grad_a, grad_b, grad_c, handed_one, handed_two, by_one, by_two, by_three):
@@ -173,17 +203,21 @@
     by_one[...] = grad_a[...]
 
 
+def sum_kernel(*refs):
+    refs[-1][...] = sum(r[...].astype(jnp.float32) for r in refs[:-1]).astype(refs[-1].dtype)
+
+
 def final_kernel(values, upstream, grad):
     unit, inverse = unit_rows(values)
     grad[...] = inverse * (upstream - unit * jnp.sum(unit * upstream, axis=-1, keepdims=True))
 
 
-def image_final_kernel(lane, images, own, far, across, near, grad, loss_rows, values, sem):
+def image_final_kernel(lane, images, own, far, grad, loss_rows, values, sem):
     n = TOK_DEV
     at = pl.ds(pl.multiple_of(lane[0] * n, n), n)
     copy = pltpu.make_async_copy(images.at[at], values, sem)
     copy.start()
-    parts = (own, far, across, near)
+    parts = (own, far)
     sums = sum(p[n:, :n].astype(jnp.float32) for p in parts)
     loss_rows[...] = jnp.sum(sums, axis=0, keepdims=True) / (STEPS * TOK_DEV)
     copy.wait()
@@ -191,8 +225,8 @@
     final_kernel(values[...], upstream, grad)
 
 
-def caption_final_kernel(captions, own, r3, r2, r1, grad):
-    upstream = own[...] + sum(r[...].astype(jnp.float32) for r in (r1, r2, r3))
+def caption_final_kernel(captions, own, r3, r4, r2, r1, grad):
+    upstream = own[...] + sum(r[...].astype(jnp.float32) for r in (r1, r2, r3, r4))
     final_kernel(captions[...], upstream, grad)
 
 
@@ -228,7 +262,8 @@
     back = [
         shift(1),
         shift(2),
-        shift(3) + crossing([(ROW - 1, 1), (ROW - 2, 0), (ROW - 3, 2)]),
+        shift(3),
+        crossing([(ROW - 1, 1), (ROW - 2, 0), (ROW - 3, 2)]),
     ]
     return forward, back, inside([(0, 1), (1, 0)]), inside([(1, 2)]), inside([(2, 1), (0, 2)])
 
@@ -280,23 +315,39 @@
         [pltpu.VMEM((n, width), wide)],
     )
     share = shape((n + PAD, width), short)
-    across, near, far, own, ga, gb, to_swap = call(
-        last_kernel,
-        (share, share, share, shape((n + PAD, width), wide), block, block, block),
+    scalars = (lane, place, logit_scale, logit_bias)
+    square = shape((n, n), short)
+    slope_shape = pltpu.VMEM((n, n), short)
+    first_share, va, vb, slope_a, slope_b = call(
+        head_kernel,
+        (share, block, block, square, square),
         [smem()] * 4 + [vmem()] * 9 + [anywhere()] * 2,
-        8 * flops,
-        "last_pairs",
-        (lane, place, logit_scale, logit_bias, image_bf, v0, f1, f2, vc, y1, y2, f5, loss, s0, sc),
-        [pltpu.VMEM((rows, n), short)] * 4
-        + [pltpu.VMEM((n, width), short)] * 2
+        3 * flops,
+        "head_pairs",
+        (*scalars, image_bf, v0, f1, f2, vc, y1, y2, f5, loss, s0, sc),
+        [slope_shape, slope_shape, pltpu.SemaphoreType.DMA((2,))],
+    )
+    far, near, own, ga, gb, to_swap = call(
+        tail_kernel,
+        (share, share, shape((n + PAD, width), wide), block, block, block),
+        [smem()] * 4 + [vmem()] * 8 + [anywhere()] * 2,
+        6 * flops,
+        "tail_pairs",
+        (*scalars, image_bf, v0, va, vb, vc, slope_a, slope_b, loss, s0, sc),
+        [pltpu.VMEM((rows, n), short)] * 2
         + [pltpu.VMEM((n, width), wide)] * 2
-        + [pltpu.VMEM((1, rows), wide), pltpu.SemaphoreType.DMA((2,))],
-    )
+        + [pltpu.SemaphoreType.DMA((2,))],
+    )
+    beside = [(0, 1), (1, 0), (2, 3), (3, 2)]
+    halves = within(first_share, beside)
+    r3 = send_back(gc, back[2])
     y1 = send(to_swap, swap)
     y2 = send(gb, pass_back)
+    far, r3 = lax.optimization_barrier((far, r3))
+    far = call(sum_kernel, share, [vmem()] * 2, 1000, "add_halves", (far, halves))
+    far, gc = lax.optimization_barrier((far, gc))
     far = within(far, [(0, 2), (1, 3), (2, 0), (3, 1)])
-    across = within(across, [(0, 3), (1, 2), (2, 1), (3, 0)])
-    near = within(near, [(0, 1), (1, 0), (2, 3), (3, 2)])
+    near = within(near, beside)
     ga, gb, gc = call(
         back_kernel,
         (block,) * 3,
@@ -305,25 +356,29 @@
         "back_sums",
         (place, ga, gb, gc, y1, y2),
     )
-    r3 = send_back(gc, back[2])
+    own, gc = lax.optimization_barrier((own, gc))
+    own = call(
+        sum_kernel, shape((n + PAD, width), wide), [vmem()] * 2, NEAR_FLOPS, "add_near", (own, near)
+    )
+    r4 = send_back(gc, back[3])
     r2 = send_back(gb, back[1])
     r1 = send_back(ga, back[0])
     image_grad, loss_rows = call(
         image_final_kernel,
         (shape((n, width), wide), shape((1, n), wide)),
-        [smem(), anywhere()] + [vmem()] * 4,
+        [smem(), anywhere()] + [vmem()] * 2,
         1000,
         "image_final",
-        (lane, images, own, far, across, near),
+        (lane, images, own, far),
         [pltpu.VMEM((n, width), short), pltpu.SemaphoreType.DMA],
     )
     caption_grad = call(
         caption_final_kernel,
         shape((n, width), wide),
-        [vmem()] * 5,
+        [vmem()] * 6,
         1000,
         "caption_final",
-        (captions, g0, r3, r2, r1),
+        (captions, g0, r3, r4, r2, r1),
     )
     return (image_grad, caption_grad, loss_rows.reshape(n))
 

time: 102 us -> 94.8 us (0.929)
  waiting for transfers between devices: 43.4 us -> 34 us
  local copies, waits for them, and re-layouts: 6.59 us -> 3.27 us
  Pallas kernels: 13.4 us -> 16.3 us
  starting transfers between devices: 35.7 us -> 38 us
    ppermute x3, waiting for transfers between devices: 23.4 us -> 15.9 us  [within(): lax.ppermute(block, AXES, [(b * n_group + s, b * n_group + t) for b in ra...]
    unnamed x18 -> x8, local copies, waits for them, and re-layouts: 5.78 us -> 2.46 us
    pallas_call x7 -> x10, Pallas kernels: 13.4 us -> 16.3 us  [call(): pl.pallas_call(kernel, out_shape=outs, in_specs=ins, out_specs=jax.tree.m...]
    ppermute x8, waiting for transfers between devices: 20 us -> 18 us  [send(): return lax.ppermute(block, AXES, route)]
    ppermute x8, starting transfers between devices: 19.5 us -> 21.5 us  [send(): return lax.ppermute(block, AXES, route)]
    ppermute x3 -> x4, starting transfers between devices: 5.88 us -> 7.04 us  [send_back(): return lax.ppermute(block, AXES, [(t, s) for s, t in route])]
  transfers between devices with their start and end apart: 14 -> 15, of which waited for: 4 -> 4; matrix products, arithmetic and copies ran while one was open for 1% -> 1% of each run, Pallas kernels for 5% -> 16%
where the time goes in v3:
time: 94.8 us; the launch traced here: 93.7 us
  starting transfers between devices  38 us (40%)
  waiting for transfers between devices  34 us (36%)
  Pallas kernels  16.3 us (17%)
  local copies, waits for them, and re-layouts  3.27 us (3%)
  between operations  2.21 us (2%)
    ppermute x8, starting transfers between devices, send(): return lax.ppermute(block, AXES, route)  21.5 us
    ppermute x8, waiting for transfers between devices, send(): return lax.ppermute(block, AXES, route)  18 us
    pallas_call x10, Pallas kernels, call(): pl.pallas_call(kernel, out_shape=outs, in_specs=ins, out_specs=jax.tree.m...  16.3 us
    ppermute x3, waiting for transfers between devices, within(): lax.ppermute(block, AXES, [(b * n_group + s, b * n_group + t) for b in ra...  15.9 us
    ppermute x3, starting transfers between devices, within(): lax.ppermute(block, AXES, [(b * n_group + s, b * n_group + t) for b in ra...  9.45 us
    ppermute x4, starting transfers between devices, send_back(): return lax.ppermute(block, AXES, [(t, s) for s, t in route])  7.04 us
    unnamed x8, local copies, waits for them, and re-layouts  2.46 us
  transfers between devices with their start and end apart: 15, of which 4 were waited for; matrix products, arithmetic and copies ran while one was open for 1% of the time, Pallas kernels for 16%

profile of v3, /device:TPU:1, one launch (start us, length us, event | category | flops | bytes accessed | tf_op | source)
XLA Modules:
  0.0 93.7 jit_solution(2757964471391272346)
XLA Ops:
  0.6 0.0 copy-start.2
  0.6 1.0 %copy-done.2 = bf16[256,768]{1,0:T(8,128)(2,1)S(1)} copy-done((bf16[256,768]{1,0:T(8,128)(2,1)S(1)}, bf16[256,768]{1,0:T(8,128)(2,1)}, u32[]{:S(2)}) %copy-start.2) | copy-done | bytes 393240
  1.6 0.2 caption_unit.1.visiting.v0
  1.8 6.0 %collective-permute-start.2 = (bf16[256,768]{1,0:T(8,128)(2,1)S(1)}, bf16[256,768]{1,0:T(8,128)(2,1)}, u32[]{:S(2)}, u32[]{:S(2)}) collective-permute-start(bf16[256,768]{1,0:T(8,128)(2,1)S(1)} %caption_unit.1.visiting.v0), channel_id=1, source_target_pairs={{0,12},{4,16},{8,20},{12,24},{16,28},{1,13},{5,17},{9,21},{13,25},... | collective-permute-start | bytes 1179656 | tf_op jit(solution)/shard_map/ppermute | solution.py:281
  7.8 1.4 %collective-permute-start.5 = (bf16[256,768]{1,0:T(8,128)(2,1)S(1)}, bf16[256,768]{1,0:T(8,128)(2,1)}, u32[]{:S(2)}, u32[]{:S(2)}) collective-permute-start(bf16[256,768]{1,0:T(8,128)(2,1)S(1)} %caption_unit.1.visiting.v0), channel_id=1, source_target_pairs={{20,35},{21,34},{22,33},{23,32},{52,67},{53,66},{54,65},{55,64},{8... | collective-permute-start | bytes 1179656 | tf_op jit(solution)/shard_map/ppermute | solution.py:281
  9.3 3.0 %collective-permute-start.1 = (bf16[256,768]{1,0:T(8,128)(2,1)S(1)}, bf16[256,768]{1,0:T(8,128)(2,1)}, u32[]{:S(2)}, u32[]{:S(2)}) collective-permute-start(bf16[256,768]{1,0:T(8,128)(2,1)S(1)} %caption_unit.1.visiting.v0), channel_id=1, source_target_pairs={{0,8},{4,12},{8,16},{12,20},{16,24},{20,28},{1,9},{5,13},{9,17},{1... | collective-permute-start | bytes 1179656 | tf_op jit(solution)/shard_map/ppermute | solution.py:281
  12.2 1.9 %collective-permute-start = (bf16[256,768]{1,0:T(8,128)(2,1)S(1)}, bf16[256,768]{1,0:T(8,128)(2,1)}, u32[]{:S(2)}, u32[]{:S(2)}) collective-permute-start(bf16[256,768]{1,0:T(8,128)(2,1)S(1)} %caption_unit.1.visiting.v0), channel_id=1, source_target_pairs={{0,4},{4,8},{8,12},{12,16},{16,20},{20,24},{24,28},{1,5},{5,9},{9,... | collective-permute-start | bytes 1179656 | tf_op jit(solution)/shard_map/ppermute | solution.py:281
  15.4 0.8 copy.8.pairing
  16.2 0.0 copy-start
  16.3 1.4 %copy-done = bf16[1024,768]{1,0:T(8,128)(2,1)S(1)} copy-done((bf16[1024,768]{1,0:T(8,128)(2,1)S(1)}, bf16[1024,768]{1,0:T(8,128)(2,1)}, u32[]{:S(2)}) %copy-start) | copy-done | bytes 1572888
  17.7 2.2 %first_pairs.1 = (bf16[1024,768]{1,0:T(8,128)(2,1)S(1)}, f32[1,1024]{1,0:T(1,128)S(1)}, bf16[1024,256]{1,0:T(8,128)(2,1)S(1)}, f32[256,768]{1,0:T(8,128)S(1)}) custom-call(bf16[1024,768]{1,0:T(8,128)(2,1)S(1)} %copy-done, bf16[256,768]{1,0:T(8,128)(2,1)S(1)} %caption_unit.1.visiting.v0, s32[256,1]{1,0:T(8,128)S(1)} %copy.8.pairing, f32[1]{0:T(128)S(6)} %copy.9.scale, ...), custom_call_target="tpu_custom_call" | custom-call | flops 805306368 | bytes 4194304 | tf_op jit(solution)/shard_map/first_pairs/pallas_call | solution.py:31
  19.8 17.3 %collective-permute-done.2.f3 = bf16[256,768]{1,0:T(8,128)(2,1)} collective-permute-done((bf16[256,768]{1,0:T(8,128)(2,1)S(1)}, bf16[256,768]{1,0:T(8,128)(2,1)}, u32[]{:S(2)}, u32[]{:S(2)}) %collective-permute-start.2) | collective-permute-done | bytes 393248 | tf_op jit(solution)/shard_map/ppermute | solution.py:281
  37.2 2.1 %collective-permute-start.4 = (bf16[256,768]{1,0:T(8,128)(2,1)}, bf16[256,768]{1,0:T(8,128)(2,1)}, u32[]{:S(2)}, u32[]{:S(2)}) collective-permute-start(bf16[256,768]{1,0:T(8,128)(2,1)} %collective-permute-done.2.f3), channel_id=1, source_target_pairs={{4,8},{5,9},{6,10},{7,11},{36,40},{37,41},{38,42},{39,43},{68,72},... | collective-permute-start | bytes 1179656 | tf_op jit(solution)/shard_map/ppermute | solution.py:281
  39.2 3.6 %collective-permute-start.3 = (bf16[256,768]{1,0:T(8,128)(2,1)}, bf16[256,768]{1,0:T(8,128)(2,1)}, u32[]{:S(2)}, u32[]{:S(2)}) collective-permute-start(bf16[256,768]{1,0:T(8,128)(2,1)} %collective-permute-done.2.f3), channel_id=1, source_target_pairs={{0,4},{4,0},{1,5},{5,1},{2,6},{6,2},{3,7},{7,3},{32,36},{36,32},{3... | collective-permute-start | bytes 1179656 | tf_op jit(solution)/shard_map/ppermute | solution.py:281
  42.9 0.0 collective-permute-done.1.f2
  42.9 2.7 %next_pairs.1 = (f32[1,1024]{1,0:T(1,128)S(1)}, bf16[1024,256]{1,0:T(8,128)(2,1)S(1)}, bf16[256,768]{1,0:T(8,128)(2,1)S(1)}, bf16[256,768]{1,0:T(8,128)(2,1)S(1)}) custom-call(s32[1]{0:T(128)} %bitcast.1.place, bf16[1024,768]{1,0:T(8,128)(2,1)S(1)} %get-tuple-element.35.image_bf, bf16[256,768]{1,0:T(8,128)(2,1)} %collective-permute-done.1.f2, ...), custom_call_target="tpu_custom_call" | custom-call | flops 805306368 | bytes 4194304 | tf_op jit(solution)/shard_map/next_pairs/pallas_call | solution.py:31
  45.6 1.3 %collective-permute-start.6 = (bf16[256,768]{1,0:T(8,128)(2,1)S(1)}, bf16[256,768]{1,0:T(8,128)(2,1)S(1)}, u32[]{:S(2)}, u32[]{:S(2)}) collective-permute-start(bf16[256,768]{1,0:T(8,128)(2,1)S(1)} %get-tuple-element.54.grad_c), channel_id=1, source_target_pairs={{12,0},{16,4},{20,8},{24,12},{28,16},{13,1},{17,5},{21,9},{25,13},... | collective-permute-start | bytes 1179656 | tf_op jit(solution)/shard_map/ppermute | solution.py:284
  46.9 0.0 collective-permute-done.5.f5
  46.9 0.0 collective-permute-done.f1
  46.9 0.0 collective-permute-done.4.y2
  46.9 0.0 collective-permute-done.3.y1
  47.0 3.3 %head_pairs.1 = (bf16[272,768]{1,0:T(8,128)(2,1)S(1)}, bf16[256,768]{1,0:T(8,128)(2,1)S(1)}, bf16[256,768]{1,0:T(8,128)(2,1)S(1)}, bf16[256,256]{1,0:T(8,128)(2,1)S(1)}, bf16[256,256]{1,0:T(8,128)(2,1)S(1)}) custom-call(s32[1]{0:T(128)} %bitcast.lane, s32[1]{0:T(128)} %bitcast.1.place, f32[1]{0:T(128)S(6)} %copy.9.scale, f32[1]{0:T(128)S(6)} %copy.10.bias, ...), custom_call_target="tpu_custom_call" | custom-call | flops 1207959552 | bytes 4194304 | tf_op jit(solution)/shard_map/head_pairs/pallas_call | solution.py:31
  50.3 4.2 %collective-permute-start.7 = (bf16[272,768]{1,0:T(8,128)(2,1)S(1)}, bf16[272,768]{1,0:T(8,128)(2,1)S(1)}, u32[]{:S(2)}, u32[]{:S(2)}) collective-permute-start(bf16[272,768]{1,0:T(8,128)(2,1)S(1)} %get-tuple-element.53), channel_id=1, source_target_pairs={{0,1},{1,0},{2,3},{3,2},{4,5},{5,4},{6,7},{7,6},{8,9},{9,8},{10,11... | collective-permute-start | bytes 1253384 | tf_op jit(solution)/shard_map/ppermute | solution.py:287
  54.5 4.8 %tail_pairs.1 = (bf16[272,768]{1,0:T(8,128)(2,1)S(1)}, bf16[272,768]{1,0:T(8,128)(2,1)S(1)}, f32[272,768]{1,0:T(8,128)S(1)}, bf16[256,768]{1,0:T(8,128)(2,1)S(1)...) custom-call(s32[1]{0:T(128)} %bitcast.lane, s32[1]{0:T(128)} %bitcast.1.place, f32[1]{0:T(128)S(6)} %copy.9.scale, ...), custom_call_target="tpu_custom_call" | custom-call | flops 2415919104 | bytes 4194304 | tf_op jit(solution)/shard_map/tail_pairs/pallas_call | solution.py:31
  59.3 2.2 %collective-permute-start.8 = (bf16[256,768]{1,0:T(8,128)(2,1)S(1)}, bf16[256,768]{1,0:T(8,128)(2,1)S(1)}, u32[]{:S(2)}, u32[]{:S(2)}) collective-permute-start(bf16[256,768]{1,0:T(8,128)(2,1)S(1)} %get-tuple-element.55), channel_id=1, source_target_pairs={{0,4},{4,0},{1,5},{5,1},{2,6},{6,2},{3,7},{7,3},{32,36},{36,32},{3... | collective-permute-start | bytes 1179656 | tf_op jit(solution)/shard_map/ppermute | solution.py:281
  61.5 1.3 %collective-permute-start.9 = (bf16[256,768]{1,0:T(8,128)(2,1)S(1)}, bf16[256,768]{1,0:T(8,128)(2,1)S(1)}, u32[]{:S(2)}, u32[]{:S(2)}) collective-permute-start(bf16[256,768]{1,0:T(8,128)(2,1)S(1)} %get-tuple-element.49.grad_b), channel_id=1, source_target_pairs={{8,4},{0,8},{9,5},{1,9},{10,6},{2,10},{11,7},{3,11},{40,36},{32,40... | collective-permute-start | bytes 1179656 | tf_op jit(solution)/shard_map/ppermute | solution.py:281
  62.8 1.9 %collective-permute-start.10 = (bf16[272,768]{1,0:T(8,128)(2,1)S(1)}, bf16[272,768]{1,0:T(8,128)(2,1)S(1)}, u32[]{:S(2)}, u32[]{:S(2)}) collective-permute-start(bf16[272,768]{1,0:T(8,128)(2,1)S(1)} %get-tuple-element.58), channel_id=1, source_target_pairs={{0,1},{1,0},{2,3},{3,2},{4,5},{5,4},{6,7},{7,6},{8,9},{9,8},{10,11... | collective-permute-start | bytes 1253384 | tf_op jit(solution)/shard_map/ppermute | solution.py:287
  64.8 0.0 collective-permute-done.6.r3
  64.8 2.0 %collective-permute-done.7.refs_1_ = bf16[272,768]{1,0:T(8,128)(2,1)S(1)} collective-permute-done((bf16[272,768]{1,0:T(8,128)(2,1)S(1)}, bf16[272,768]{1,0:T(8,128)(2,1)S(1)}, u32[]{:S(2)}, u32[]{:S(2)}) %collective-permute-start.7) | collective-permute-done | bytes 417824 | tf_op jit(solution)/shard_map/ppermute | solution.py:287
  66.8 0.1 add_halves.1
  66.9 3.3 %collective-permute-start.11 = (bf16[272,768]{1,0:T(8,128)(2,1)S(1)}, bf16[272,768]{1,0:T(8,128)(2,1)S(1)}, u32[]{:S(2)}, u32[]{:S(2)}) collective-permute-start(bf16[272,768]{1,0:T(8,128)(2,1)S(1)} %add_halves.1), channel_id=1, source_target_pairs={{0,2},{1,3},{2,0},{3,1},{4,6},{5,7},{6,4},{7,5},{8,10},{9,11},{10,... | collective-permute-start | bytes 1253384 | tf_op jit(solution)/shard_map/ppermute | solution.py:287
  70.2 0.0 collective-permute-done.8.handed_one
  70.2 0.7 collective-permute-done.9.handed_two
  70.9 0.2 back_sums.1
  71.1 1.3 %collective-permute-start.12 = (bf16[256,768]{1,0:T(8,128)(2,1)S(1)}, bf16[256,768]{1,0:T(8,128)(2,1)S(1)}, u32[]{:S(2)}, u32[]{:S(2)}) collective-permute-start(bf16[256,768]{1,0:T(8,128)(2,1)S(1)} %get-tuple-element.63), channel_id=1, source_target_pairs={{39,28},{35,24},{43,20},{38,29},{34,25},{42,21},{37,30},{33,26},{4... | collective-permute-start | bytes 1179656 | tf_op jit(solution)/shard_map/ppermute | solution.py:284
  72.4 1.3 %collective-permute-start.13 = (bf16[256,768]{1,0:T(8,128)(2,1)S(1)}, bf16[256,768]{1,0:T(8,128)(2,1)S(1)}, u32[]{:S(2)}, u32[]{:S(2)}) collective-permute-start(bf16[256,768]{1,0:T(8,128)(2,1)S(1)} %get-tuple-element.64), channel_id=1, source_target_pairs={{8,0},{12,4},{16,8},{20,12},{24,16},{28,20},{9,1},{13,5},{17,9},{2... | collective-permute-start | bytes 1179656 | tf_op jit(solution)/shard_map/ppermute | solution.py:284
  73.7 0.0 copy-start.3
  73.8 3.1 %collective-permute-start.14 = (bf16[256,768]{1,0:T(8,128)(2,1)S(1)}, bf16[256,768]{1,0:T(8,128)(2,1)S(1)}, u32[]{:S(2)}, u32[]{:S(2)}) collective-permute-start(bf16[256,768]{1,0:T(8,128)(2,1)S(1)} %get-tuple-element.65), channel_id=1, source_target_pairs={{4,0},{8,4},{12,8},{16,12},{20,16},{24,20},{28,24},{5,1},{9,5},{13... | collective-permute-start | bytes 1179656 | tf_op jit(solution)/shard_map/ppermute | solution.py:284
  76.9 13.9 %collective-permute-done.10.refs_1_ = bf16[272,768]{1,0:T(8,128)(2,1)S(1)} collective-permute-done((bf16[272,768]{1,0:T(8,128)(2,1)S(1)}, bf16[272,768]{1,0:T(8,128)(2,1)S(1)}, u32[]{:S(2)}, u32[]{:S(2)}) %collective-permute-start.10) | collective-permute-done | bytes 417824 | tf_op jit(solution)/shard_map/ppermute | solution.py:287
  90.8 0.1 add_near.1.own
  90.9 0.0 collective-permute-done.12.r4
  90.9 0.0 collective-permute-done.13.r2
  90.9 0.0 collective-permute-done.14.r1
  90.9 0.0 copy-start.1
  90.9 1.3 %caption_final.1 = f32[256,768]{1,0:T(8,128)} custom-call(bf16[256,768]{1,0:T(8,128)(2,1)S(1)} %copy-done.3, f32[256,768]{1,0:T(8,128)S(1)} %get-tuple-element.61.own, bf16[256,768]{1,0:T(8,128)(2,1)S(1)} %collective-permute-done.6.r3, bf16[256,768]{1,0:T(8,128)(2,1)S(1)} %collective-permute-done.12.r4, bf16[256,768]{1,0:T(8,128)(2,1)S(1)} %collective-permute-done.13.r2, ...), custom_call_target="tpu_custom_call" | custom-call | flops 1000 | bytes 4194304 | tf_op jit(solution)/shard_map/caption_final/pallas_call | solution.py:31
  92.3 0.0 collective-permute-done.11.far
  92.3 0.1 copy-done.1
  92.3 1.4 %image_final.1 = (f32[256,768]{1,0:T(8,128)}, f32[1,256]{1,0:T(1,128)}) custom-call(s32[1]{0:T(128)} %bitcast.lane, bf16[1024,768]{1,0:T(8,128)(2,1)S(1)} %copy-done.1, f32[272,768]{1,0:T(8,128)S(1)} %add_near.1.own, bf16[272,768]{1,0:T(8,128)(2,1)S(1)} %collective-permute-done.11.far), custom_call_target="tpu_custom_call" | custom-call | flops 1000 | bytes 4194304 | tf_op jit(solution)/shard_map/image_final/pallas_call | solution.py:31
  (1 shorter events, 0.0 us)
Async XLA Ops:
  0.6 1.0 %copy-start.2 = (bf16[256,768]{1,0:T(8,128)(2,1)S(1)}, bf16[256,768]{1,0:T(8,128)(2,1)}, u32[]{:S(2)}) copy-start(bf16[256,768]{1,0:T(8,128)(2,1)} %captions.3) | copy-start | bytes 1179652
  1.8 35.4 %collective-permute-start.2 = (bf16[256,768]{1,0:T(8,128)(2,1)S(1)}, bf16[256,768]{1,0:T(8,128)(2,1)}, u32[]{:S(2)}, u32[]{:S(2)}) collective-permute-start(bf16[256,768]{1,0:T(8,128)(2,1)S(1)} %caption_unit.1.visiting.v0), channel_id=1, source_target_pairs={{0,12},{4,16},{8,20},{12,24},{16,28},{1,13},{5,17},{9,21},{13,25},... | collective-permute-start | bytes 1179656 | tf_op jit(solution)/shard_map/ppermute | solution.py:281
  7.8 39.1 %collective-permute-start.5 = (bf16[256,768]{1,0:T(8,128)(2,1)S(1)}, bf16[256,768]{1,0:T(8,128)(2,1)}, u32[]{:S(2)}, u32[]{:S(2)}) collective-permute-start(bf16[256,768]{1,0:T(8,128)(2,1)S(1)} %caption_unit.1.visiting.v0), channel_id=1, source_target_pairs={{20,35},{21,34},{22,33},{23,32},{52,67},{53,66},{54,65},{55,64},{8... | collective-permute-start | bytes 1179656 | tf_op jit(solution)/shard_map/ppermute | solution.py:281
  9.3 33.6 %collective-permute-start.1 = (bf16[256,768]{1,0:T(8,128)(2,1)S(1)}, bf16[256,768]{1,0:T(8,128)(2,1)}, u32[]{:S(2)}, u32[]{:S(2)}) collective-permute-start(bf16[256,768]{1,0:T(8,128)(2,1)S(1)} %caption_unit.1.visiting.v0), channel_id=1, source_target_pairs={{0,8},{4,12},{8,16},{12,20},{16,24},{20,28},{1,9},{5,13},{9,17},{1... | collective-permute-start | bytes 1179656 | tf_op jit(solution)/shard_map/ppermute | solution.py:281
  12.2 34.7 %collective-permute-start = (bf16[256,768]{1,0:T(8,128)(2,1)S(1)}, bf16[256,768]{1,0:T(8,128)(2,1)}, u32[]{:S(2)}, u32[]{:S(2)}) collective-permute-start(bf16[256,768]{1,0:T(8,128)(2,1)S(1)} %caption_unit.1.visiting.v0), channel_id=1, source_target_pairs={{0,4},{4,8},{8,12},{12,16},{16,20},{20,24},{24,28},{1,5},{5,9},{9,... | collective-permute-start | bytes 1179656 | tf_op jit(solution)/shard_map/ppermute | solution.py:281
  16.2 1.4 %copy-start = (bf16[1024,768]{1,0:T(8,128)(2,1)S(1)}, bf16[1024,768]{1,0:T(8,128)(2,1)}, u32[]{:S(2)}) copy-start(bf16[1024,768]{1,0:T(8,128)(2,1)} %images.3) | copy-start | bytes 4718596
  37.2 9.8 %collective-permute-start.4 = (bf16[256,768]{1,0:T(8,128)(2,1)}, bf16[256,768]{1,0:T(8,128)(2,1)}, u32[]{:S(2)}, u32[]{:S(2)}) collective-permute-start(bf16[256,768]{1,0:T(8,128)(2,1)} %collective-permute-done.2.f3), channel_id=1, source_target_pairs={{4,8},{5,9},{6,10},{7,11},{36,40},{37,41},{38,42},{39,43},{68,72},... | collective-permute-start | bytes 1179656 | tf_op jit(solution)/shard_map/ppermute | solution.py:281
  39.2 7.7 %collective-permute-start.3 = (bf16[256,768]{1,0:T(8,128)(2,1)}, bf16[256,768]{1,0:T(8,128)(2,1)}, u32[]{:S(2)}, u32[]{:S(2)}) collective-permute-start(bf16[256,768]{1,0:T(8,128)(2,1)} %collective-permute-done.2.f3), channel_id=1, source_target_pairs={{0,4},{4,0},{1,5},{5,1},{2,6},{6,2},{3,7},{7,3},{32,36},{36,32},{3... | collective-permute-start | bytes 1179656 | tf_op jit(solution)/shard_map/ppermute | solution.py:281
  45.6 19.1 %collective-permute-start.6 = (bf16[256,768]{1,0:T(8,128)(2,1)S(1)}, bf16[256,768]{1,0:T(8,128)(2,1)S(1)}, u32[]{:S(2)}, u32[]{:S(2)}) collective-permute-start(bf16[256,768]{1,0:T(8,128)(2,1)S(1)} %get-tuple-element.54.grad_c), channel_id=1, source_target_pairs={{12,0},{16,4},{20,8},{24,12},{28,16},{13,1},{17,5},{21,9},{25,13},... | collective-permute-start | bytes 1179656 | tf_op jit(solution)/shard_map/ppermute | solution.py:284
  50.3 16.5 %collective-permute-start.7 = (bf16[272,768]{1,0:T(8,128)(2,1)S(1)}, bf16[272,768]{1,0:T(8,128)(2,1)S(1)}, u32[]{:S(2)}, u32[]{:S(2)}) collective-permute-start(bf16[272,768]{1,0:T(8,128)(2,1)S(1)} %get-tuple-element.53), channel_id=1, source_target_pairs={{0,1},{1,0},{2,3},{3,2},{4,5},{5,4},{6,7},{7,6},{8,9},{9,8},{10,11... | collective-permute-start | bytes 1253384 | tf_op jit(solution)/shard_map/ppermute | solution.py:287
  59.3 10.9 %collective-permute-start.8 = (bf16[256,768]{1,0:T(8,128)(2,1)S(1)}, bf16[256,768]{1,0:T(8,128)(2,1)S(1)}, u32[]{:S(2)}, u32[]{:S(2)}) collective-permute-start(bf16[256,768]{1,0:T(8,128)(2,1)S(1)} %get-tuple-element.55), channel_id=1, source_target_pairs={{0,4},{4,0},{1,5},{5,1},{2,6},{6,2},{3,7},{7,3},{32,36},{36,32},{3... | collective-permute-start | bytes 1179656 | tf_op jit(solution)/shard_map/ppermute | solution.py:281
  61.5 9.4 %collective-permute-start.9 = (bf16[256,768]{1,0:T(8,128)(2,1)S(1)}, bf16[256,768]{1,0:T(8,128)(2,1)S(1)}, u32[]{:S(2)}, u32[]{:S(2)}) collective-permute-start(bf16[256,768]{1,0:T(8,128)(2,1)S(1)} %get-tuple-element.49.grad_b), channel_id=1, source_target_pairs={{8,4},{0,8},{9,5},{1,9},{10,6},{2,10},{11,7},{3,11},{40,36},{32,40... | collective-permute-start | bytes 1179656 | tf_op jit(solution)/shard_map/ppermute | solution.py:281
  62.8 28.0 %collective-permute-start.10 = (bf16[272,768]{1,0:T(8,128)(2,1)S(1)}, bf16[272,768]{1,0:T(8,128)(2,1)S(1)}, u32[]{:S(2)}, u32[]{:S(2)}) collective-permute-start(bf16[272,768]{1,0:T(8,128)(2,1)S(1)} %get-tuple-element.58), channel_id=1, source_target_pairs={{0,1},{1,0},{2,3},{3,2},{4,5},{5,4},{6,7},{7,6},{8,9},{9,8},{10,11... | collective-permute-start | bytes 1253384 | tf_op jit(solution)/shard_map/ppermute | solution.py:287
  66.9 25.4 %collective-permute-start.11 = (bf16[272,768]{1,0:T(8,128)(2,1)S(1)}, bf16[272,768]{1,0:T(8,128)(2,1)S(1)}, u32[]{:S(2)}, u32[]{:S(2)}) collective-permute-start(bf16[272,768]{1,0:T(8,128)(2,1)S(1)} %add_halves.1), channel_id=1, source_target_pairs={{0,2},{1,3},{2,0},{3,1},{4,6},{5,7},{6,4},{7,5},{8,10},{9,11},{10,... | collective-permute-start | bytes 1253384 | tf_op jit(solution)/shard_map/ppermute | solution.py:287
  71.1 19.8 %collective-permute-start.12 = (bf16[256,768]{1,0:T(8,128)(2,1)S(1)}, bf16[256,768]{1,0:T(8,128)(2,1)S(1)}, u32[]{:S(2)}, u32[]{:S(2)}) collective-permute-start(bf16[256,768]{1,0:T(8,128)(2,1)S(1)} %get-tuple-element.63), channel_id=1, source_target_pairs={{39,28},{35,24},{43,20},{38,29},{34,25},{42,21},{37,30},{33,26},{4... | collective-permute-start | bytes 1179656 | tf_op jit(solution)/shard_map/ppermute | solution.py:284
  72.4 18.5 %collective-permute-start.13 = (bf16[256,768]{1,0:T(8,128)(2,1)S(1)}, bf16[256,768]{1,0:T(8,128)(2,1)S(1)}, u32[]{:S(2)}, u32[]{:S(2)}) collective-permute-start(bf16[256,768]{1,0:T(8,128)(2,1)S(1)} %get-tuple-element.64), channel_id=1, source_target_pairs={{8,0},{12,4},{16,8},{20,12},{24,16},{28,20},{9,1},{13,5},{17,9},{2... | collective-permute-start | bytes 1179656 | tf_op jit(solution)/shard_map/ppermute | solution.py:284
  73.7 17.2 %copy-start.3 = (bf16[256,768]{1,0:T(8,128)(2,1)S(1)}, bf16[256,768]{1,0:T(8,128)(2,1)}, u32[]{:S(2)}) copy-start(bf16[256,768]{1,0:T(8,128)(2,1)} %captions.3) | copy-start | bytes 1179652
  73.8 17.2 %collective-permute-start.14 = (bf16[256,768]{1,0:T(8,128)(2,1)S(1)}, bf16[256,768]{1,0:T(8,128)(2,1)S(1)}, u32[]{:S(2)}, u32[]{:S(2)}) collective-permute-start(bf16[256,768]{1,0:T(8,128)(2,1)S(1)} %get-tuple-element.65), channel_id=1, source_target_pairs={{4,0},{8,4},{12,8},{16,12},{20,16},{24,20},{28,24},{5,1},{9,5},{13... | collective-permute-start | bytes 1179656 | tf_op jit(solution)/shard_map/ppermute | solution.py:284
  90.9 1.4 %copy-start.1 = (bf16[1024,768]{1,0:T(8,128)(2,1)S(1)}, bf16[1024,768]{1,0:T(8,128)(2,1)}, u32[]{:S(2)}) copy-start(bf16[1024,768]{1,0:T(8,128)(2,1)} %images.3) | copy-start | bytes 4718596

commit v4 on v3

--- a/solution.py
+++ b/solution.py
@@ -10,7 +10,7 @@
 AXES = ("blk", "group")
 ROW = 8
 PAD = 16
-NEAR_FLOPS = 1 * 10**9
+NEAR_FLOPS = 12 * 10**9
 VMEM_BYTES = 16 * 1024 * 1024
 NT = (((1,), (1,)), ((), ()))
 
@@ -212,12 +212,12 @@
     grad[...] = inverse * (upstream - unit * jnp.sum(unit * upstream, axis=-1, keepdims=True))
 
 
-def image_final_kernel(lane, images, own, far, grad, loss_rows, values, sem):
+def image_final_kernel(lane, images, own, far, near, grad, loss_rows, values, sem):
     n = TOK_DEV
     at = pl.ds(pl.multiple_of(lane[0] * n, n), n)
     copy = pltpu.make_async_copy(images.at[at], values, sem)
     copy.start()
-    parts = (own, far)
+    parts = (own, far, near)
     sums = sum(p[n:, :n].astype(jnp.float32) for p in parts)
     loss_rows[...] = jnp.sum(sums, axis=0, keepdims=True) / (STEPS * TOK_DEV)
     copy.wait()
@@ -341,11 +341,11 @@
     beside = [(0, 1), (1, 0), (2, 3), (3, 2)]
     halves = within(first_share, beside)
     r3 = send_back(gc, back[2])
+    far, r3 = lax.optimization_barrier((far, r3))
+    far = call(sum_kernel, share, [vmem()] * 2, 1000, "add_halves", (far, halves))
+    far, gb, gc, to_swap = lax.optimization_barrier((far, gb, gc, to_swap))
     y1 = send(to_swap, swap)
     y2 = send(gb, pass_back)
-    far, r3 = lax.optimization_barrier((far, r3))
-    far = call(sum_kernel, share, [vmem()] * 2, 1000, "add_halves", (far, halves))
-    far, gc = lax.optimization_barrier((far, gc))
     far = within(far, [(0, 2), (1, 3), (2, 0), (3, 1)])
     near = within(near, beside)
     ga, gb, gc = call(
@@ -356,20 +356,16 @@
         "back_sums",
         (place, ga, gb, gc, y1, y2),
     )
-    own, gc = lax.optimization_barrier((own, gc))
-    own = call(
-        sum_kernel, shape((n + PAD, width), wide), [vmem()] * 2, NEAR_FLOPS, "add_near", (own, near)
-    )
     r4 = send_back(gc, back[3])
     r2 = send_back(gb, back[1])
     r1 = send_back(ga, back[0])
     image_grad, loss_rows = call(
         image_final_kernel,
         (shape((n, width), wide), shape((1, n), wide)),
-        [smem(), anywhere()] + [vmem()] * 2,
-        1000,
+        [smem(), anywhere()] + [vmem()] * 3,
+        NEAR_FLOPS,
         "image_final",
-        (lane, images, own, far),
+        (lane, images, own, far, near),
         [pltpu.VMEM((n, width), short), pltpu.SemaphoreType.DMA],
     )
     caption_grad = call(

time: 94.8 us -> 101 us (1.065)
  waiting for transfers between devices: 34 us -> 40.8 us
    ppermute x3, waiting for transfers between devices: 15.9 us -> 6.97 us  [within(): lax.ppermute(block, AXES, [(b * n_group + s, b * n_group + t) for b in ra...]
    ppermute x4, waiting for transfers between devices: 0.01 us -> 8.37 us  [send_back(): return lax.ppermute(block, AXES, [(t, s) for s, t in route])]
    ppermute x8, waiting for transfers between devices: 18 us -> 25.4 us  [send(): return lax.ppermute(block, AXES, route)]
    ppermute x3, starting transfers between devices: 9.45 us -> 11.1 us  [within(): lax.ppermute(block, AXES, [(b * n_group + s, b * n_group + t) for b in ra...]
    ppermute x4, starting transfers between devices: 7.04 us -> 5.82 us  [send_back(): return lax.ppermute(block, AXES, [(t, s) for s, t in route])]
    pallas_call x10 -> x9, Pallas kernels: 16.3 us -> 16.3 us  [call(): pl.pallas_call(kernel, out_shape=outs, in_specs=ins, out_specs=jax.tree.m...]
  transfers between devices with their start and end apart: 15 -> 15, of which waited for: 4 -> 8; matrix products, arithmetic and copies ran while one was open for 1% -> 1% of each run, Pallas kernels for 16% -> 11%
where the time goes in v4:
time: 101 us
  waiting for transfers between devices  40.8 us (40%)
  starting transfers between devices  38.1 us (38%)
  Pallas kernels  16.3 us (16%)
  local copies, waits for them, and re-layouts  3.21 us (3%)
  between operations  2.17 us (2%)
    ppermute x8, waiting for transfers between devices, send(): return lax.ppermute(block, AXES, route)  25.4 us
    ppermute x8, starting transfers between devices, send(): return lax.ppermute(block, AXES, route)  21.2 us
    pallas_call x9, Pallas kernels, call(): pl.pallas_call(kernel, out_shape=outs, in_specs=ins, out_specs=jax.tree.m...  16.3 us
    ppermute x3, starting transfers between devices, within(): lax.ppermute(block, AXES, [(b * n_group + s, b * n_group + t) for b in ra...  11.1 us
    ppermute x4, waiting for transfers between devices, send_back(): return lax.ppermute(block, AXES, [(t, s) for s, t in route])  8.37 us
    ppermute x3, waiting for transfers between devices, within(): lax.ppermute(block, AXES, [(b * n_group + s, b * n_group + t) for b in ra...  6.97 us
    ppermute x4, starting transfers between devices, send_back(): return lax.ppermute(block, AXES, [(t, s) for s, t in route])  5.82 us
    unnamed x8, local copies, waits for them, and re-layouts  2.4 us
  transfers between devices with their start and end apart: 15, of which 8 were waited for; matrix products, arithmetic and copies ran while one was open for 1% of the time, Pallas kernels for 11%

profile of v4, /device:TPU:1, one launch (start us, length us, event | category | flops | bytes accessed | tf_op | source)
XLA Modules:
  0.0 100.6 jit_solution(15733136536101355839)
XLA Ops:
  0.6 0.0 copy-start
  0.6 1.0 copy-done
  1.6 0.2 caption_unit.1.visiting.v0
  1.8 6.0 %collective-permute-start.2 = (bf16[256,768]{1,0:T(8,128)(2,1)S(1)}, bf16[256,768]{1,0:T(8,128)(2,1)}, u32[]{:S(2)}, u32[]{:S(2)}) collective-permute-start(bf16[256,768]{1,0:T(8,128)(2,1)S(1)} %caption_unit.1.visiting.v0), channel_id=1, source_target_pairs={{0,12},{4,16},{8,20},{12,24},{16,28},{1,13},{5,17},{9,21},{13,25},... | collective-permute-start | bytes 1179656 | tf_op jit(solution)/shard_map/ppermute | solution.py:281
  7.8 1.4 %collective-permute-start.5 = (bf16[256,768]{1,0:T(8,128)(2,1)S(1)}, bf16[256,768]{1,0:T(8,128)(2,1)}, u32[]{:S(2)}, u32[]{:S(2)}) collective-permute-start(bf16[256,768]{1,0:T(8,128)(2,1)S(1)} %caption_unit.1.visiting.v0), channel_id=1, source_target_pairs={{20,35},{21,34},{22,33},{23,32},{52,67},{53,66},{54,65},{55,64},{8... | collective-permute-start | bytes 1179656 | tf_op jit(solution)/shard_map/ppermute | solution.py:281
  9.3 3.0 %collective-permute-start.1 = (bf16[256,768]{1,0:T(8,128)(2,1)S(1)}, bf16[256,768]{1,0:T(8,128)(2,1)}, u32[]{:S(2)}, u32[]{:S(2)}) collective-permute-start(bf16[256,768]{1,0:T(8,128)(2,1)S(1)} %caption_unit.1.visiting.v0), channel_id=1, source_target_pairs={{0,8},{4,12},{8,16},{12,20},{16,24},{20,28},{1,9},{5,13},{9,17},{1... | collective-permute-start | bytes 1179656 | tf_op jit(solution)/shard_map/ppermute | solution.py:281
  12.2 1.9 %collective-permute-start = (bf16[256,768]{1,0:T(8,128)(2,1)S(1)}, bf16[256,768]{1,0:T(8,128)(2,1)}, u32[]{:S(2)}, u32[]{:S(2)}) collective-permute-start(bf16[256,768]{1,0:T(8,128)(2,1)S(1)} %caption_unit.1.visiting.v0), channel_id=1, source_target_pairs={{0,4},{4,8},{8,12},{12,16},{16,20},{20,24},{24,28},{1,5},{5,9},{9,... | collective-permute-start | bytes 1179656 | tf_op jit(solution)/shard_map/ppermute | solution.py:281
  15.4 0.8 copy.8.pairing
  16.2 0.0 copy-start.2
  16.3 1.4 %copy-done.2 = bf16[1024,768]{1,0:T(8,128)(2,1)S(1)} copy-done((bf16[1024,768]{1,0:T(8,128)(2,1)S(1)}, bf16[1024,768]{1,0:T(8,128)(2,1)}, u32[]{:S(2)}) %copy-start.2) | copy-done | bytes 1572888
  17.7 2.2 %first_pairs.1 = (bf16[1024,768]{1,0:T(8,128)(2,1)S(1)}, f32[1,1024]{1,0:T(1,128)S(1)}, bf16[1024,256]{1,0:T(8,128)(2,1)S(1)}, f32[256,768]{1,0:T(8,128)S(1)}) custom-call(bf16[1024,768]{1,0:T(8,128)(2,1)S(1)} %copy-done.2, bf16[256,768]{1,0:T(8,128)(2,1)S(1)} %caption_unit.1.visiting.v0, s32[256,1]{1,0:T(8,128)S(1)} %copy.8.pairing, f32[1]{0:T(128)S(6)} %copy.9.scale, ...), custom_call_target="tpu_custom_call" | custom-call | flops 805306368 | bytes 4194304 | tf_op jit(solution)/shard_map/first_pairs/pallas_call | solution.py:31
  19.8 17.3 %collective-permute-done.2.f3 = bf16[256,768]{1,0:T(8,128)(2,1)} collective-permute-done((bf16[256,768]{1,0:T(8,128)(2,1)S(1)}, bf16[256,768]{1,0:T(8,128)(2,1)}, u32[]{:S(2)}, u32[]{:S(2)}) %collective-permute-start.2) | collective-permute-done | bytes 393248 | tf_op jit(solution)/shard_map/ppermute | solution.py:281
  37.2 2.1 %collective-permute-start.4 = (bf16[256,768]{1,0:T(8,128)(2,1)}, bf16[256,768]{1,0:T(8,128)(2,1)}, u32[]{:S(2)}, u32[]{:S(2)}) collective-permute-start(bf16[256,768]{1,0:T(8,128)(2,1)} %collective-permute-done.2.f3), channel_id=1, source_target_pairs={{4,8},{5,9},{6,10},{7,11},{36,40},{37,41},{38,42},{39,43},{68,72},... | collective-permute-start | bytes 1179656 | tf_op jit(solution)/shard_map/ppermute | solution.py:281
  39.2 3.6 %collective-permute-start.3 = (bf16[256,768]{1,0:T(8,128)(2,1)}, bf16[256,768]{1,0:T(8,128)(2,1)}, u32[]{:S(2)}, u32[]{:S(2)}) collective-permute-start(bf16[256,768]{1,0:T(8,128)(2,1)} %collective-permute-done.2.f3), channel_id=1, source_target_pairs={{0,4},{4,0},{1,5},{5,1},{2,6},{6,2},{3,7},{7,3},{32,36},{36,32},{3... | collective-permute-start | bytes 1179656 | tf_op jit(solution)/shard_map/ppermute | solution.py:281
  42.9 0.0 collective-permute-done.1.f2
  42.9 2.7 %next_pairs.1 = (f32[1,1024]{1,0:T(1,128)S(1)}, bf16[1024,256]{1,0:T(8,128)(2,1)S(1)}, bf16[256,768]{1,0:T(8,128)(2,1)S(1)}, bf16[256,768]{1,0:T(8,128)(2,1)S(1)}) custom-call(s32[1]{0:T(128)} %bitcast.1.place, bf16[1024,768]{1,0:T(8,128)(2,1)S(1)} %get-tuple-element.35.image_bf, bf16[256,768]{1,0:T(8,128)(2,1)} %collective-permute-done.1.f2, ...), custom_call_target="tpu_custom_call" | custom-call | flops 805306368 | bytes 4194304 | tf_op jit(solution)/shard_map/next_pairs/pallas_call | solution.py:31
  45.6 0.0 collective-permute-done.5.f5
  45.6 0.0 collective-permute-done.f1
  45.6 0.0 collective-permute-done.4.y2
  45.6 0.0 collective-permute-done.3.y1
  45.7 3.3 %head_pairs.1 = (bf16[272,768]{1,0:T(8,128)(2,1)S(1)}, bf16[256,768]{1,0:T(8,128)(2,1)S(1)}, bf16[256,768]{1,0:T(8,128)(2,1)S(1)}, bf16[256,256]{1,0:T(8,128)(2,1)S(1)}, bf16[256,256]{1,0:T(8,128)(2,1)S(1)}) custom-call(s32[1]{0:T(128)} %bitcast.lane, s32[1]{0:T(128)} %bitcast.1.place, f32[1]{0:T(128)S(6)} %copy.9.scale, f32[1]{0:T(128)S(6)} %copy.10.bias, ...), custom_call_target="tpu_custom_call" | custom-call | flops 1207959552 | bytes 4194304 | tf_op jit(solution)/shard_map/head_pairs/pallas_call | solution.py:31
  49.0 4.3 %collective-permute-start.7 = (bf16[272,768]{1,0:T(8,128)(2,1)S(1)}, bf16[272,768]{1,0:T(8,128)(2,1)S(1)}, u32[]{:S(2)}, u32[]{:S(2)}) collective-permute-start(bf16[272,768]{1,0:T(8,128)(2,1)S(1)} %get-tuple-element.51), channel_id=1, source_target_pairs={{0,1},{1,0},{2,3},{3,2},{4,5},{5,4},{6,7},{7,6},{8,9},{9,8},{10,11... | collective-permute-start | bytes 1253384 | tf_op jit(solution)/shard_map/ppermute | solution.py:287
  53.3 1.3 %collective-permute-start.6 = (bf16[256,768]{1,0:T(8,128)(2,1)S(1)}, bf16[256,768]{1,0:T(8,128)(2,1)S(1)}, u32[]{:S(2)}, u32[]{:S(2)}) collective-permute-start(bf16[256,768]{1,0:T(8,128)(2,1)S(1)} %get-tuple-element.61.grad_c), channel_id=1, source_target_pairs={{12,0},{16,4},{20,8},{24,12},{28,16},{13,1},{17,5},{21,9},{25,13},... | collective-permute-start | bytes 1179656 | tf_op jit(solution)/shard_map/ppermute | solution.py:284
  54.6 4.8 %tail_pairs.1 = (bf16[272,768]{1,0:T(8,128)(2,1)S(1)}, bf16[272,768]{1,0:T(8,128)(2,1)S(1)}, f32[272,768]{1,0:T(8,128)S(1)}, bf16[256,768]{1,0:T(8,128)(2,1)S(1)...) custom-call(s32[1]{0:T(128)} %bitcast.lane, s32[1]{0:T(128)} %bitcast.1.place, f32[1]{0:T(128)S(6)} %copy.9.scale, ...), custom_call_target="tpu_custom_call" | custom-call | flops 2415919104 | bytes 4194304 | tf_op jit(solution)/shard_map/tail_pairs/pallas_call | solution.py:31
  59.4 4.5 %collective-permute-done.6.r3 = bf16[256,768]{1,0:T(8,128)(2,1)S(1)} collective-permute-done((bf16[256,768]{1,0:T(8,128)(2,1)S(1)}, bf16[256,768]{1,0:T(8,128)(2,1)S(1)}, u32[]{:S(2)}, u32[]{:S(2)}) %collective-permute-start.6) | collective-permute-done | bytes 393248 | tf_op jit(solution)/shard_map/ppermute | solution.py:284
  63.9 0.0 copy-start.3
  63.9 2.0 %collective-permute-start.9 = (bf16[272,768]{1,0:T(8,128)(2,1)S(1)}, bf16[272,768]{1,0:T(8,128)(2,1)S(1)}, u32[]{:S(2)}, u32[]{:S(2)}) collective-permute-start(bf16[272,768]{1,0:T(8,128)(2,1)S(1)} %get-tuple-element.55), channel_id=1, source_target_pairs={{0,1},{1,0},{2,3},{3,2},{4,5},{5,4},{6,7},{7,6},{8,9},{9,8},{10,11... | collective-permute-start | bytes 1253384 | tf_op jit(solution)/shard_map/ppermute | solution.py:287
  65.9 0.0 collective-permute-done.7.refs_1_
  65.9 0.1 add_halves.1
  66.0 4.8 %collective-permute-start.8 = (bf16[272,768]{1,0:T(8,128)(2,1)S(1)}, bf16[272,768]{1,0:T(8,128)(2,1)S(1)}, u32[]{:S(2)}, u32[]{:S(2)}) collective-permute-start(bf16[272,768]{1,0:T(8,128)(2,1)S(1)} %add_halves.1), channel_id=1, source_target_pairs={{0,2},{1,3},{2,0},{3,1},{4,6},{5,7},{6,4},{7,5},{8,10},{9,11},{10,... | collective-permute-start | bytes 1253384 | tf_op jit(solution)/shard_map/ppermute | solution.py:287
  70.8 1.9 %collective-permute-start.10 = (bf16[256,768]{1,0:T(8,128)(2,1)S(1)}, bf16[256,768]{1,0:T(8,128)(2,1)S(1)}, u32[]{:S(2)}, u32[]{:S(2)}) collective-permute-start(bf16[256,768]{1,0:T(8,128)(2,1)S(1)} %get-tuple-element.62), channel_id=1, source_target_pairs={{0,4},{4,0},{1,5},{5,1},{2,6},{6,2},{3,7},{7,3},{32,36},{36,32},{3... | collective-permute-start | bytes 1179656 | tf_op jit(solution)/shard_map/ppermute | solution.py:281
  72.7 1.3 %collective-permute-start.11 = (bf16[256,768]{1,0:T(8,128)(2,1)S(1)}, bf16[256,768]{1,0:T(8,128)(2,1)S(1)}, u32[]{:S(2)}, u32[]{:S(2)}) collective-permute-start(bf16[256,768]{1,0:T(8,128)(2,1)S(1)} %get-tuple-element.60.grad_b), channel_id=1, source_target_pairs={{8,4},{0,8},{9,5},{1,9},{10,6},{2,10},{11,7},{3,11},{40,36},{32,40... | collective-permute-start | bytes 1179656 | tf_op jit(solution)/shard_map/ppermute | solution.py:281
  74.0 0.4 collective-permute-done.10.handed_one
  74.4 7.7 %collective-permute-done.11.handed_two = bf16[256,768]{1,0:T(8,128)(2,1)S(1)} collective-permute-done((bf16[256,768]{1,0:T(8,128)(2,1)S(1)}, bf16[256,768]{1,0:T(8,128)(2,1)S(1)}, u32[]{:S(2)}, u32[]{:S(2)}) %collective-permute-start.11) | collective-permute-done | bytes 393248 | tf_op jit(solution)/shard_map/ppermute | solution.py:281
  82.1 0.2 back_sums.1
  82.4 1.3 %collective-permute-start.12 = (bf16[256,768]{1,0:T(8,128)(2,1)S(1)}, bf16[256,768]{1,0:T(8,128)(2,1)S(1)}, u32[]{:S(2)}, u32[]{:S(2)}) collective-permute-start(bf16[256,768]{1,0:T(8,128)(2,1)S(1)} %get-tuple-element.63), channel_id=1, source_target_pairs={{39,28},{35,24},{43,20},{38,29},{34,25},{42,21},{37,30},{33,26},{4... | collective-permute-start | bytes 1179656 | tf_op jit(solution)/shard_map/ppermute | solution.py:284
  83.7 1.3 %collective-permute-start.13 = (bf16[256,768]{1,0:T(8,128)(2,1)S(1)}, bf16[256,768]{1,0:T(8,128)(2,1)S(1)}, u32[]{:S(2)}, u32[]{:S(2)}) collective-permute-start(bf16[256,768]{1,0:T(8,128)(2,1)S(1)} %get-tuple-element.64), channel_id=1, source_target_pairs={{8,0},{12,4},{16,8},{20,12},{24,16},{28,20},{9,1},{13,5},{17,9},{2... | collective-permute-start | bytes 1179656 | tf_op jit(solution)/shard_map/ppermute | solution.py:284
  85.0 1.9 %collective-permute-start.14 = (bf16[256,768]{1,0:T(8,128)(2,1)S(1)}, bf16[256,768]{1,0:T(8,128)(2,1)S(1)}, u32[]{:S(2)}, u32[]{:S(2)}) collective-permute-start(bf16[256,768]{1,0:T(8,128)(2,1)S(1)} %get-tuple-element.65), channel_id=1, source_target_pairs={{4,0},{8,4},{12,8},{16,12},{20,16},{24,20},{28,24},{5,1},{9,5},{13... | collective-permute-start | bytes 1179656 | tf_op jit(solution)/shard_map/ppermute | solution.py:284
  86.9 7.0 %collective-permute-done.9.near = bf16[272,768]{1,0:T(8,128)(2,1)S(1)} collective-permute-done((bf16[272,768]{1,0:T(8,128)(2,1)S(1)}, bf16[272,768]{1,0:T(8,128)(2,1)S(1)}, u32[]{:S(2)}, u32[]{:S(2)}) %collective-permute-start.9) | collective-permute-done | bytes 417824 | tf_op jit(solution)/shard_map/ppermute | solution.py:287
  93.9 0.0 collective-permute-done.8.far
  93.9 0.0 copy-done.3
  93.9 0.0 copy-start.1
  93.9 1.5 %image_final.1 = (f32[256,768]{1,0:T(8,128)}, f32[1,256]{1,0:T(1,128)}) custom-call(s32[1]{0:T(128)} %bitcast.lane, bf16[1024,768]{1,0:T(8,128)(2,1)S(1)} %copy-done.3, f32[272,768]{1,0:T(8,128)S(1)} %get-tuple-element.47.own, bf16[272,768]{1,0:T(8,128)(2,1)S(1)} %collective-permute-done.8.far, bf16[272,768]{1,0:T(8,128)(2,1)S(1)} %collective-permute-done.9.near), custom_call_target="tpu_custom_call" | custom-call | flops 12000000000 | bytes 4194304 | tf_op jit(solution)/shard_map/image_final/pallas_call | solution.py:31
  95.4 0.9 collective-permute-done.12.r4
  96.3 0.2 collective-permute-done.13.r2
  96.5 2.8 %collective-permute-done.14.r1 = bf16[256,768]{1,0:T(8,128)(2,1)S(1)} collective-permute-done((bf16[256,768]{1,0:T(8,128)(2,1)S(1)}, bf16[256,768]{1,0:T(8,128)(2,1)S(1)}, u32[]{:S(2)}, u32[]{:S(2)}) %collective-permute-start.14) | collective-permute-done | bytes 393248 | tf_op jit(solution)/shard_map/ppermute | solution.py:284
  99.2 0.0 copy-done.1
  99.2 1.4 %caption_final.1 = f32[256,768]{1,0:T(8,128)} custom-call(bf16[256,768]{1,0:T(8,128)(2,1)S(1)} %copy-done.1, f32[256,768]{1,0:T(8,128)S(1)} %get-tuple-element.57.own, bf16[256,768]{1,0:T(8,128)(2,1)S(1)} %collective-permute-done.6.r3, bf16[256,768]{1,0:T(8,128)(2,1)S(1)} %collective-permute-done.12.r4, bf16[256,768]{1,0:T(8,128)(2,1)S(1)} %collective-permute-done.13.r2, ...), custom_call_target="tpu_custom_call" | custom-call | flops 1000 | bytes 4194304 | tf_op jit(solution)/shard_map/caption_final/pallas_call | solution.py:31
Async XLA Ops:
  0.6 1.0 copy-start
  1.8 35.4 %collective-permute-start.2 = (bf16[256,768]{1,0:T(8,128)(2,1)S(1)}, bf16[256,768]{1,0:T(8,128)(2,1)}, u32[]{:S(2)}, u32[]{:S(2)}) collective-permute-start(bf16[256,768]{1,0:T(8,128)(2,1)S(1)} %caption_unit.1.visiting.v0), channel_id=1, source_target_pairs={{0,12},{4,16},{8,20},{12,24},{16,28},{1,13},{5,17},{9,21},{13,25},... | collective-permute-start | bytes 1179656 | tf_op jit(solution)/shard_map/ppermute | solution.py:281
  7.8 37.8 %collective-permute-start.5 = (bf16[256,768]{1,0:T(8,128)(2,1)S(1)}, bf16[256,768]{1,0:T(8,128)(2,1)}, u32[]{:S(2)}, u32[]{:S(2)}) collective-permute-start(bf16[256,768]{1,0:T(8,128)(2,1)S(1)} %caption_unit.1.visiting.v0), channel_id=1, source_target_pairs={{20,35},{21,34},{22,33},{23,32},{52,67},{53,66},{54,65},{55,64},{8... | collective-permute-start | bytes 1179656 | tf_op jit(solution)/shard_map/ppermute | solution.py:281
  9.3 33.6 %collective-permute-start.1 = (bf16[256,768]{1,0:T(8,128)(2,1)S(1)}, bf16[256,768]{1,0:T(8,128)(2,1)}, u32[]{:S(2)}, u32[]{:S(2)}) collective-permute-start(bf16[256,768]{1,0:T(8,128)(2,1)S(1)} %caption_unit.1.visiting.v0), channel_id=1, source_target_pairs={{0,8},{4,12},{8,16},{12,20},{16,24},{20,28},{1,9},{5,13},{9,17},{1... | collective-permute-start | bytes 1179656 | tf_op jit(solution)/shard_map/ppermute | solution.py:281
  12.2 33.4 %collective-permute-start = (bf16[256,768]{1,0:T(8,128)(2,1)S(1)}, bf16[256,768]{1,0:T(8,128)(2,1)}, u32[]{:S(2)}, u32[]{:S(2)}) collective-permute-start(bf16[256,768]{1,0:T(8,128)(2,1)S(1)} %caption_unit.1.visiting.v0), channel_id=1, source_target_pairs={{0,4},{4,8},{8,12},{12,16},{16,20},{20,24},{24,28},{1,5},{5,9},{9,... | collective-permute-start | bytes 1179656 | tf_op jit(solution)/shard_map/ppermute | solution.py:281
  16.2 1.4 %copy-start.2 = (bf16[1024,768]{1,0:T(8,128)(2,1)S(1)}, bf16[1024,768]{1,0:T(8,128)(2,1)}, u32[]{:S(2)}) copy-start(bf16[1024,768]{1,0:T(8,128)(2,1)} %images.3) | copy-start | bytes 4718596
  37.2 8.5 %collective-permute-start.4 = (bf16[256,768]{1,0:T(8,128)(2,1)}, bf16[256,768]{1,0:T(8,128)(2,1)}, u32[]{:S(2)}, u32[]{:S(2)}) collective-permute-start(bf16[256,768]{1,0:T(8,128)(2,1)} %collective-permute-done.2.f3), channel_id=1, source_target_pairs={{4,8},{5,9},{6,10},{7,11},{36,40},{37,41},{38,42},{39,43},{68,72},... | collective-permute-start | bytes 1179656 | tf_op jit(solution)/shard_map/ppermute | solution.py:281
  39.2 6.4 %collective-permute-start.3 = (bf16[256,768]{1,0:T(8,128)(2,1)}, bf16[256,768]{1,0:T(8,128)(2,1)}, u32[]{:S(2)}, u32[]{:S(2)}) collective-permute-start(bf16[256,768]{1,0:T(8,128)(2,1)} %collective-permute-done.2.f3), channel_id=1, source_target_pairs={{0,4},{4,0},{1,5},{5,1},{2,6},{6,2},{3,7},{7,3},{32,36},{36,32},{3... | collective-permute-start | bytes 1179656 | tf_op jit(solution)/shard_map/ppermute | solution.py:281
  49.0 16.9 %collective-permute-start.7 = (bf16[272,768]{1,0:T(8,128)(2,1)S(1)}, bf16[272,768]{1,0:T(8,128)(2,1)S(1)}, u32[]{:S(2)}, u32[]{:S(2)}) collective-permute-start(bf16[272,768]{1,0:T(8,128)(2,1)S(1)} %get-tuple-element.51), channel_id=1, source_target_pairs={{0,1},{1,0},{2,3},{3,2},{4,5},{5,4},{6,7},{7,6},{8,9},{9,8},{10,11... | collective-permute-start | bytes 1253384 | tf_op jit(solution)/shard_map/ppermute | solution.py:287
  53.3 10.6 %collective-permute-start.6 = (bf16[256,768]{1,0:T(8,128)(2,1)S(1)}, bf16[256,768]{1,0:T(8,128)(2,1)S(1)}, u32[]{:S(2)}, u32[]{:S(2)}) collective-permute-start(bf16[256,768]{1,0:T(8,128)(2,1)S(1)} %get-tuple-element.61.grad_c), channel_id=1, source_target_pairs={{12,0},{16,4},{20,8},{24,12},{28,16},{13,1},{17,5},{21,9},{25,13},... | collective-permute-start | bytes 1179656 | tf_op jit(solution)/shard_map/ppermute | solution.py:284
  63.9 30.0 %copy-start.3 = (bf16[1024,768]{1,0:T(8,128)(2,1)S(1)}, bf16[1024,768]{1,0:T(8,128)(2,1)}, u32[]{:S(2)}) copy-start(bf16[1024,768]{1,0:T(8,128)(2,1)} %images.3) | copy-start | bytes 4718596
  63.9 30.0 %collective-permute-start.9 = (bf16[272,768]{1,0:T(8,128)(2,1)S(1)}, bf16[272,768]{1,0:T(8,128)(2,1)S(1)}, u32[]{:S(2)}, u32[]{:S(2)}) collective-permute-start(bf16[272,768]{1,0:T(8,128)(2,1)S(1)} %get-tuple-element.55), channel_id=1, source_target_pairs={{0,1},{1,0},{2,3},{3,2},{4,5},{5,4},{6,7},{7,6},{8,9},{9,8},{10,11... | collective-permute-start | bytes 1253384 | tf_op jit(solution)/shard_map/ppermute | solution.py:287
  66.0 27.8 %collective-permute-start.8 = (bf16[272,768]{1,0:T(8,128)(2,1)S(1)}, bf16[272,768]{1,0:T(8,128)(2,1)S(1)}, u32[]{:S(2)}, u32[]{:S(2)}) collective-permute-start(bf16[272,768]{1,0:T(8,128)(2,1)S(1)} %add_halves.1), channel_id=1, source_target_pairs={{0,2},{1,3},{2,0},{3,1},{4,6},{5,7},{6,4},{7,5},{8,10},{9,11},{10,... | collective-permute-start | bytes 1253384 | tf_op jit(solution)/shard_map/ppermute | solution.py:287
  70.8 3.6 %collective-permute-start.10 = (bf16[256,768]{1,0:T(8,128)(2,1)S(1)}, bf16[256,768]{1,0:T(8,128)(2,1)S(1)}, u32[]{:S(2)}, u32[]{:S(2)}) collective-permute-start(bf16[256,768]{1,0:T(8,128)(2,1)S(1)} %get-tuple-element.62), channel_id=1, source_target_pairs={{0,4},{4,0},{1,5},{5,1},{2,6},{6,2},{3,7},{7,3},{32,36},{36,32},{3... | collective-permute-start | bytes 1179656 | tf_op jit(solution)/shard_map/ppermute | solution.py:281
  72.7 9.4 %collective-permute-start.11 = (bf16[256,768]{1,0:T(8,128)(2,1)S(1)}, bf16[256,768]{1,0:T(8,128)(2,1)S(1)}, u32[]{:S(2)}, u32[]{:S(2)}) collective-permute-start(bf16[256,768]{1,0:T(8,128)(2,1)S(1)} %get-tuple-element.60.grad_b), channel_id=1, source_target_pairs={{8,4},{0,8},{9,5},{1,9},{10,6},{2,10},{11,7},{3,11},{40,36},{32,40... | collective-permute-start | bytes 1179656 | tf_op jit(solution)/shard_map/ppermute | solution.py:281
  82.4 13.9 %collective-permute-start.12 = (bf16[256,768]{1,0:T(8,128)(2,1)S(1)}, bf16[256,768]{1,0:T(8,128)(2,1)S(1)}, u32[]{:S(2)}, u32[]{:S(2)}) collective-permute-start(bf16[256,768]{1,0:T(8,128)(2,1)S(1)} %get-tuple-element.63), channel_id=1, source_target_pairs={{39,28},{35,24},{43,20},{38,29},{34,25},{42,21},{37,30},{33,26},{4... | collective-permute-start | bytes 1179656 | tf_op jit(solution)/shard_map/ppermute | solution.py:284
  83.7 12.8 %collective-permute-start.13 = (bf16[256,768]{1,0:T(8,128)(2,1)S(1)}, bf16[256,768]{1,0:T(8,128)(2,1)S(1)}, u32[]{:S(2)}, u32[]{:S(2)}) collective-permute-start(bf16[256,768]{1,0:T(8,128)(2,1)S(1)} %get-tuple-element.64), channel_id=1, source_target_pairs={{8,0},{12,4},{16,8},{20,12},{24,16},{28,20},{9,1},{13,5},{17,9},{2... | collective-permute-start | bytes 1179656 | tf_op jit(solution)/shard_map/ppermute | solution.py:284
  85.0 14.3 %collective-permute-start.14 = (bf16[256,768]{1,0:T(8,128)(2,1)S(1)}, bf16[256,768]{1,0:T(8,128)(2,1)S(1)}, u32[]{:S(2)}, u32[]{:S(2)}) collective-permute-start(bf16[256,768]{1,0:T(8,128)(2,1)S(1)} %get-tuple-element.65), channel_id=1, source_target_pairs={{4,0},{8,4},{12,8},{16,12},{20,16},{24,20},{28,24},{5,1},{9,5},{13... | collective-permute-start | bytes 1179656 | tf_op jit(solution)/shard_map/ppermute | solution.py:284
  93.9 5.4 %copy-start.1 = (bf16[256,768]{1,0:T(8,128)(2,1)S(1)}, bf16[256,768]{1,0:T(8,128)(2,1)}, u32[]{:S(2)}) copy-start(bf16[256,768]{1,0:T(8,128)(2,1)} %captions.3) | copy-start | bytes 1179652
